TPU v7x, 512 devices: a whole 4x4x16 slice. The times are simulated.
512 devices in a mesh: ri: 16 (over z_hi, x), rj: 32 (over z_lo, y, core).
Axes of the slice: x: 4, y: 4, z: 16 (z_hi: 4, z_lo: 4; z = z_hi * 4 + z_lo), core: 2. Of those that a mesh axis runs over, the one named last changes fastest.
Arguments:
- couple_sensitivity: bfloat16 [512, 512, 128], P('ri', 'rj'), may hold values from -6 to 6
- stored_first_halves: bfloat16 [512, 4096], P('ri', 'rj'), may hold values from -6 to 6
- stored_second_halves: bfloat16 [512, 4096], P('ri', 'rj'), may hold values from -6 to 6
- incoming_sensitivity: bfloat16 [512, 128, 256], P('ri', 'rj'), may hold values from -6 to 6
- homolog_activations: bfloat16 [512, 128, 256], P('ri', 'rj'), may hold values from -4 to 4
- tensor_couple_map: bfloat16 [1024, 128], replicated, may hold values from -0.5 to 0.5
- homolog_to_half_map: bfloat16 [256, 64], replicated, may hold values from -0.75 to 0.75
- query_key_value_gate_map: bfloat16 [256, 1024], replicated, may hold values from -0.375 to 0.375
- attended_result_map: bfloat16 [256, 256], replicated, may hold values from -0.75 to 0.75
Outputs:
- msa_grad_out: bfloat16 [512, 128, 256], P('ri', 'rj')
All inputs are finite; a program needn't handle non-finite values.
Results may differ from a plain program's by a relative error of at most 0.009.
Values may be sent and summed in bfloat16 or wider, within the bound.
No kernel may reach another device: no remote copies, remote signals or barrier semaphores. Data moves between devices by JAX's collectives and lax.ppermute only.
A program may use at most 64 MiB of HBM per device.

v0:
```python
import jax
import jax.numpy as jnp
from jax import lax
from jax.sharding import PartitionSpec as P

HALF_FEATURES = 32
HEADS = 8


def spread(value, axis, source):
    kept = jnp.where(lax.axis_index(axis) == source, value, 0).astype(value.dtype)
    return lax.psum(kept, axis)


def column_attention_backward(
    alignment_block, block_gradient, query_key_value_gate_map, attended_result_map
):
    amino_number, sequence_depth_rows, feature_number = alignment_block.shape
    head_size = feature_number // HEADS
    score_scale = head_size ** (-0.5)
    projected_factors = jnp.einsum(
        "tcx,xy->tcy", alignment_block, query_key_value_gate_map, preferred_element_type=jnp.float32
    ).astype(jnp.bfloat16)
    shaped = projected_factors.reshape(amino_number, sequence_depth_rows, 4, HEADS, head_size)
    queries = shaped[:, :, 0]
    key_heads = shaped[:, :, 1]
    values = shaped[:, :, 2]
    gate_logits = shaped[:, :, 3]
    scores = (
        jnp.einsum("nshd,nthd->nhst", queries, key_heads, preferred_element_type=jnp.float32)
        * score_scale
    )
    weights = jnp.exp(scores)
    attention = weights / jnp.sum(weights, axis=-1, keepdims=True)
    attention_low = attention.astype(jnp.bfloat16)
    attended = jnp.einsum(
        "nhst,nthd->nshd", attention_low, values, preferred_element_type=jnp.float32
    )
    gate_open = jax.nn.sigmoid(gate_logits.astype(jnp.float32))
    grad_gated = jnp.einsum(
        "nsm,om->nso", block_gradient, attended_result_map, preferred_element_type=jnp.float32
    ).reshape(amino_number, sequence_depth_rows, HEADS, head_size)
    grad_attended = (gate_open * grad_gated).astype(jnp.bfloat16)
    grad_logits = grad_gated * attended * gate_open * (1.0 - gate_open)
    grad_weights = jnp.einsum(
        "nshd,nthd->nhst", grad_attended, values, preferred_element_type=jnp.float32
    )
    grad_scores = (
        attention
        * (grad_weights - jnp.sum(attention * grad_weights, axis=-1, keepdims=True))
        * score_scale
    ).astype(jnp.bfloat16)
    grad_queries = jnp.einsum(
        "nhst,nthd->nshd", grad_scores, key_heads, preferred_element_type=jnp.float32
    )
    grad_keys = jnp.einsum(
        "nhst,nshd->nthd", grad_scores, queries, preferred_element_type=jnp.float32
    )
    grad_values = jnp.einsum(
        "nhst,nshd->nthd", attention_low, grad_attended, preferred_element_type=jnp.float32
    )
    projection_gradient = (
        jnp.stack([grad_queries, grad_keys, grad_values, grad_logits], axis=2)
        .reshape(amino_number, sequence_depth_rows, 4 * feature_number)
        .astype(jnp.bfloat16)
    )
    alignment_gradient = jnp.einsum(
        "eia,qa->eiq",
        projection_gradient,
        query_key_value_gate_map,
        preferred_element_type=jnp.float32,
    )
    return (block_gradient.astype(jnp.float32) + alignment_gradient).astype(jnp.bfloat16)


def local(
    couple_sensitivity,
    stored_first_halves,
    stored_second_halves,
    incoming_sensitivity,
    homolog_activations,
    tensor_couple_map,
    homolog_to_half_map,
    query_key_value_gate_map,
    attended_result_map,
):
    row_count = couple_sensitivity.shape[0]
    col_count = couple_sensitivity.shape[1]
    ri_count = lax.axis_size("ri")
    rj_count = lax.axis_size("rj")
    ri_place = lax.axis_index("ri")
    rj_place = lax.axis_index("rj")
    shard_rows = incoming_sensitivity.shape[1]
    total_rows = shard_rows * rj_count
    left_rows, right_rows = (
        lax.all_gather(stored_first_halves, "rj", axis=1, tiled=True),
        lax.all_gather(stored_second_halves, "rj", axis=1, tiled=True),
    )
    ratio = rj_count // ri_count
    column_piece = lax.dynamic_slice_in_dim(right_rows, rj_place % ratio * col_count, col_count, 0)
    right_cols = spread(column_piece, "ri", rj_place // ratio)
    right_reshaped = right_cols.reshape(col_count, total_rows, HALF_FEATURES)
    block = 16
    turns = row_count // block
    pair_block_list = couple_sensitivity.reshape(
        turns, block, col_count, couple_sensitivity.shape[2]
    )
    left_block_list = left_rows.reshape(turns, block, total_rows, HALF_FEATURES)

    def step_forward(loop_state, pieces):
        pair_piece, left_portion = pieces
        outer_product = (
            jnp.einsum(
                "ijk,fk->ijf", pair_piece, tensor_couple_map, preferred_element_type=jnp.float32
            )
            .astype(jnp.bfloat16)
            .reshape(block, col_count, HALF_FEATURES, HALF_FEATURES)
        )
        left_portion_gradient = (
            jnp.einsum(
                "altg,lbg->abt", outer_product, right_reshaped, preferred_element_type=jnp.float32
            )
            / total_rows
        )
        loop_state = (
            loop_state
            + jnp.einsum(
                "lzno,lwn->zwo", outer_product, left_portion, preferred_element_type=jnp.float32
            )
            / total_rows
        )
        return (loop_state, left_portion_gradient)

    right_part, left_stacked = lax.scan(
        step_forward,
        jnp.zeros((col_count, total_rows, HALF_FEATURES), jnp.float32),
        (pair_block_list, left_block_list),
    )
    left_part = left_stacked.reshape(row_count, total_rows * HALF_FEATURES)
    right_part = right_part.reshape(col_count, total_rows * HALF_FEATURES)
    share_width = shard_rows * HALF_FEATURES
    left_total = lax.psum(left_part, "rj")
    left_gradient = lax.dynamic_slice_in_dim(
        left_total, rj_place * share_width, share_width, 1
    ).astype(jnp.bfloat16)
    right_total = lax.psum(right_part, "ri").astype(jnp.bfloat16)
    right_home = lax.all_to_all(right_total, "rj", split_axis=1, concat_axis=0, tiled=True)
    right_gradient = lax.dynamic_slice_in_dim(right_home, ri_place * row_count, row_count, 0)
    factor_gradient = jnp.concatenate(
        [
            left_gradient.reshape(row_count, shard_rows, HALF_FEATURES),
            right_gradient.reshape(row_count, shard_rows, HALF_FEATURES),
        ],
        axis=-1,
    )
    alignment_grad_total = (
        incoming_sensitivity.astype(jnp.float32)
        + jnp.einsum(
            "whb,ib->whi", factor_gradient, homolog_to_half_map, preferred_element_type=jnp.float32
        )
    ).astype(jnp.bfloat16)
    feature_count = homolog_activations.shape[2]
    group_res = row_count // rj_count
    grouped_acts = homolog_activations.reshape(rj_count, group_res, shard_rows, feature_count)
    grouped_grads = alignment_grad_total.reshape(rj_count, group_res, shard_rows, feature_count)
    acts_piece = lax.all_to_all(grouped_acts, "rj", split_axis=0, concat_axis=2, tiled=True)
    grads_piece = lax.all_to_all(grouped_grads, "rj", split_axis=0, concat_axis=2, tiled=True)
    item_count = acts_piece.shape[1]
    result = column_attention_backward(
        acts_piece.reshape(item_count, total_rows, feature_count),
        grads_piece.reshape(item_count, total_rows, feature_count),
        query_key_value_gate_map,
        attended_result_map,
    )
    columns = result.reshape(1, item_count, total_rows, feature_count)
    returned = lax.all_to_all(columns, "rj", split_axis=2, concat_axis=0, tiled=True)
    return returned.reshape(row_count, shard_rows, feature_count)


def solution(mesh):
    return jax.shard_map(
        local,
        mesh=mesh,
        in_specs=(
            P("ri", "rj", None),
            P("ri", "rj"),
            P("ri", "rj"),
            P("ri", "rj", None),
            P("ri", "rj", None),
            P(),
            P(),
            P(),
            P(),
        ),
        out_specs=P("ri", "rj", None),
        check_vma=False,
    )
```

profile of v0, /device:TPU:1, one launch (start us, length us, event | category | flops | bytes accessed | tf_op | source)
XLA Modules:
  0.0 563.5 jit_solution(8983740682437723523)
XLA Ops:
  6.5 0.0 copy-start
  6.5 0.0 all-reduce.4.cloned.1.call-start
  6.5 47.0 %all_gather.7 = bf16[32,4096]{1,0:T(8,128)(2,1)S(1)} all-gather(bf16[32,128]{1,0:T(8,128)(2,1)} %param.13), channel_id=1, replica_groups=mesh['ri'=16,'rj'=32] {'rj'}, dimensions={1}, use_global_device_ids=true | all-gather | bytes 270336 | tf_op jit(solution)/shard_map/all_gather | solution.py:97
  53.6 1.2 reshape.200
  54.8 0.0 all-reduce.4.cloned.1.call-update
  54.8 4.5 all-to-all-start.2
  59.3 44.6 %all_gather.6 = bf16[32,4096]{1,0:T(8,128)(2,1)S(1)} all-gather(bf16[32,128]{1,0:T(8,128)(2,1)} %param.12), channel_id=1, replica_groups=mesh['ri'=16,'rj'=32] {'rj'}, dimensions={1}, use_global_device_ids=true | all-gather | bytes 270336 | tf_op jit(solution)/shard_map/all_gather | solution.py:96
  103.9 0.8 reshape.198
  104.7 1.0 copy.59
  105.8 141.5 %all-reduce.4.cloned.1.call-done = bf16[16,128,32]{2,1,0:T(8,128)(2,1)} async-done(((bf16[16,128,32]{2,1,0:T(8,128)(2,1)}), bf16[16,128,32]{2,1,0:T(8,128)(2,1)}) %all-reduce.4.cloned.1.call-update) | async-done | bytes 131088 | tf_op jit(solution)/shard_map/psum | solution.py:12
  247.3 1.9 copy.60
  249.2 0.0 copy-done.1
  249.2 11.9 %while.13 = (s32[]{:T(128)}, f32[16,128,32]{1,2,0:T(8,128)S(1)}, f32[2,16,128,32]{2,3,1,0:T(8,128)}, bf16[2,16,128,32]{2,3,1,0:T(8,128)(2,1)}, bf16[2,16,16,128]...) while((s32[]{:T(128)}, f32[16,128,32]{1,2,0:T(8,128)S(1)}, ...), condition=%wide.region_2.3_spmd.clone, body=%wide.region_1.2_spmd.clone.sunk | while | flops 201850880 | bytes 10289859 | solution.py:134
  249.2 1.2 convolution_convert_fusion.6
  250.4 1.6 reshape.232
  252.0 0.0 copy-start.2
  252.0 1.7 fusion.81
  253.8 0.5 fusion.82
  254.3 0.8 copy-done.3
  255.1 1.2 convolution_convert_fusion.6
  256.4 1.6 reshape.232
  258.0 1.7 fusion.81
  259.7 0.5 fusion.82
  260.3 0.8 copy-done.3
  261.1 0.3 copy.62
  261.4 0.5 reshape.203
  261.9 88.1 %all-reduce.6 = bf16[16,4096]{1,0:T(8,128)(2,1)S(1)} all-reduce(f32[16,4096]{1,0:T(8,128)S(1)} %reshape.203), channel_id=1, replica_groups=mesh['ri'=16,'rj'=32] {'ri'}, use_global_device_ids=true, to_apply=%region_4.5 | all-reduce | flops 65536 | bytes 393216 | tf_op jit(solution)/shard_map/psum | solution.py:146
  350.0 1.6 copy.61
  351.6 0.0 copy-start.6
  351.7 0.0 copy-start.7
  351.7 1.0 reshape.201
  352.6 0.7 copy_bitcast_fusion
  353.3 0.0 all-to-all-done.2
  353.3 31.1 %all-to-all-start = ((bf16[16,32,128]{2,0,1:T(8,128)(2,1)}), bf16[16,32,128]{2,0,1:T(8,128)(2,1)S(1)}, u32[]{:S(2)}, u32[]{:S(2)}) async-start(bf16[16,32,128]{2,0,1:T(8,128)(2,1)} %copy_bitcast_fusion), calls=%async_computation | async-start | bytes 262144 | tf_op jit(solution)/shard_map/all_to_all | solution.py:147
  384.3 137.0 %all-reduce.5 = bf16[32,4096]{1,0:T(8,128)(2,1)S(1)} all-reduce(f32[32,4096]{1,0:T(8,128)S(1)} %reshape.201), channel_id=1, replica_groups=mesh['ri'=16,'rj'=32] {'rj'}, use_global_device_ids=true, to_apply=%region_3.4 | all-reduce | flops 131072 | bytes 786432 | tf_op jit(solution)/shard_map/psum | solution.py:142
  521.4 0.1 reshape.202
  521.5 0.9 reshape.208
  522.4 0.0 all-to-all-done
  522.4 0.1 reshape.204
  522.5 0.0 copy-done.6
  522.5 0.0 copy-done.7
  522.5 0.0 copy-start.5
  522.5 0.2 fusion.29
  522.7 0.7 copy.66
  523.4 9.8 %all-to-all-start.1 = ((bf16[32,1,4,256]{3,2,1,0:T(4,128)(2,1)}), bf16[32,1,4,256]{3,2,1,0:T(4,128)(2,1)S(1)}, u32[]{:S(2)}, u32[]{:S(2)}) async-start(bf16[32,1,4,256]{3,2,1,0:T(4,128)(2,1)} %copy.66), calls=%async_computation.1 | async-start | bytes 131072 | tf_op jit(solution)/shard_map/all_to_all | solution.py:167
  533.2 0.2 convolution_convert_fusion.1
  533.5 0.2 copy.67
  533.7 0.3 fusion.37
  534.0 7.1 %all-to-all-done.1 = bf16[32,1,4,256]{3,2,1,0:T(4,128)(2,1)S(1)} async-done(((bf16[32,1,4,256]{3,2,1,0:T(4,128)(2,1)}), bf16[32,1,4,256]{3,2,1,0:T(4,128)(2,1)S(1)}, u32[]{:S(2)}, u32[]{:S(2)}) %all-to-all-start.1) | async-done | bytes 65568 | tf_op jit(solution)/shard_map/all_to_all | solution.py:167
  541.1 0.0 copy-done.5
  541.1 0.2 fusion.57
  541.3 0.3 fusion.43
  541.6 0.2 fusion.26
  541.8 0.3 fusion.27
  542.1 0.3 fusion.28
  542.4 0.2 fusion.31
  542.6 0.3 fusion.30
  542.9 0.1 copy.89
  543.1 0.5 broadcast.112
  543.6 1.0 reduce.6
  544.6 10.9 %all_to_all.46 = bf16[32,2,512]{2,1,0:T(2,128)(2,1)S(1)} all-to-all(bf16[32,2,512]{2,1,0:T(2,128)(2,1)S(1)} %reshape.229), channel_id=1, replica_groups=mesh['ri'=16,'rj'=32] {'rj'}, dimensions={0} | all-to-all | bytes 131072 | tf_op jit(solution)/shard_map/all_to_all | solution.py:176
  555.5 0.1 reshape.230
  555.6 0.4 bitcast_reduce_fusion
  556.0 0.7 reshape.216
  (21 shorter events, 0.2 us)
Async XLA Ops:
  6.5 526.7 %copy-start = (bf16[256,1024]{1,0:T(8,128)(2,1)S(1)}, bf16[256,1024]{1,0:T(8,128)(2,1)}, u32[]{:S(2)}) copy-start(bf16[256,1024]{1,0:T(8,128)(2,1)} %param.18) | copy-start | bytes 1572868
  6.5 240.8 %all-reduce.4.cloned.1.call-start = ((), (), s32[]{:S(2)}) async-start(), calls=%async_computation.4 | async-start | bytes 1048576 | tf_op jit(solution)/shard_map/psum | solution.py:12
  54.8 194.4 %copy-start.1 = (bf16[32,16,128]{2,1,0:T(8,128)(2,1)S(1)}, bf16[32,16,128]{2,1,0:T(8,128)(2,1)}, u32[]{:S(2)}) copy-start(bf16[32,16,128]{2,1,0:T(8,128)(2,1)} %param.11) | copy-start | bytes 393220
  54.8 298.5 %all-to-all-start.2 = ((bf16[32,1,4,256]{3,2,1,0:T(4,128)(2,1)}), bf16[32,1,4,256]{3,2,1,0:T(4,128)(2,1)}, u32[]{:S(2)}, u32[]{:S(2)}) async-start(bf16[32,1,4,256]{3,2,1,0:T(4,128)(2,1)} %bitcast.182), calls=%async_computation.2 | async-start | bytes 131072 | tf_op jit(solution)/shard_map/all_to_all | solution.py:166
  252.0 1.7 copy-start.2
  252.0 1.7 copy-start.4
  254.3 0.8 copy-start.3
  258.0 1.7 copy-start.2
  258.0 1.7 copy-start.4
  260.3 0.8 copy-start.3
  351.6 170.9 %copy-start.6 = (bf16[32,4,256]{2,1,0:T(4,128)(2,1)S(1)}, bf16[32,4,256]{2,1,0:T(4,128)(2,1)}, u32[]{:S(2)}) copy-start(bf16[32,4,256]{2,1,0:T(4,128)(2,1)} %param.14) | copy-start | bytes 196612
  351.7 170.9 %copy-start.7 = (bf16[256,64]{0,1:T(8,128)(2,1)S(1)}, bf16[256,64]{0,1:T(8,128)(2,1)}, u32[]{:S(2)}) copy-start(bf16[256,64]{0,1:T(8,128)(2,1)} %param.17) | copy-start | bytes 98308
  353.3 169.1 %all-to-all-start = ((bf16[16,32,128]{2,0,1:T(8,128)(2,1)}), bf16[16,32,128]{2,0,1:T(8,128)(2,1)S(1)}, u32[]{:S(2)}, u32[]{:S(2)}) async-start(bf16[16,32,128]{2,0,1:T(8,128)(2,1)} %copy_bitcast_fusion), calls=%async_computation | async-start | bytes 262144 | tf_op jit(solution)/shard_map/all_to_all | solution.py:147
  522.5 18.6 %copy-start.5 = (bf16[256,256]{1,0:T(8,128)(2,1)S(1)}, bf16[256,256]{1,0:T(8,128)(2,1)}, u32[]{:S(2)}) copy-start(bf16[256,256]{1,0:T(8,128)(2,1)} %param.19) | copy-start | bytes 393220
  523.4 17.7 %all-to-all-start.1 = ((bf16[32,1,4,256]{3,2,1,0:T(4,128)(2,1)}), bf16[32,1,4,256]{3,2,1,0:T(4,128)(2,1)S(1)}, u32[]{:S(2)}, u32[]{:S(2)}) async-start(bf16[32,1,4,256]{3,2,1,0:T(4,128)(2,1)} %copy.66), calls=%async_computation.1 | async-start | bytes 131072 | tf_op jit(solution)/shard_map/all_to_all | solution.py:167
Sparse Core Ops, SparseCore 0:
  54.9 192.3 all-reduce.3
where the time goes:
time: 564 us; the launch traced here: 563 us
  blocking collectives  328 us (58%)
  waiting for transfers between devices  149 us (26%)
  starting transfers between devices  45.4 us (8%)
  local copies, waits for them, and re-layouts  17.4 us (3%)
  between operations  13.7 us (2%)
  matrix products  9.51 us (2%)
    psum x1, waiting for transfers between devices, spread(): return lax.psum(kept, axis)  142 us
    psum x1, blocking collectives, local(): left_total = lax.psum(left_part, 'rj')  137 us
    psum x1, blocking collectives, local(): right_total = lax.psum(right_part, 'ri').astype(jnp.bfloat16)  88.1 us
    all_gather x1, blocking collectives, local(): lax.all_gather(stored_second_halves, 'rj', axis=1, tiled=True)  47 us
    all_gather x1, blocking collectives, local(): lax.all_gather(stored_first_halves, 'rj', axis=1, tiled=True)  44.6 us
    all_to_all x1, starting transfers between devices, local(): lax.all_to_all(right_total, 'rj', split_axis=1, concat_axis=0, tiled=True)  31.1 us
  transfers between devices with their start and end apart: 4, of which 2 were waited for; matrix products, arithmetic and copies ran while one was open for 3% of the time, Pallas kernels for 0%

commit v1 on v0

v1 whole, which is shorter than its diff:
```python
import jax
import jax.numpy as jnp
from jax import lax
from jax.sharding import PartitionSpec as P

HALF = 32
HEADS = 8


def attention_backward(acts, grad, qkvg_map, result_map):
    rows, features = acts.shape
    head = features // HEADS
    scale = head ** (-0.5)
    projected = jnp.einsum(
        "cx,xy->cy", acts, qkvg_map, preferred_element_type=jnp.float32
    ).astype(jnp.bfloat16)
    shaped = projected.reshape(rows, 4, HEADS, head)
    queries, keys, values, logits = shaped[:, 0], shaped[:, 1], shaped[:, 2], shaped[:, 3]
    scores = jnp.einsum("shd,thd->hst", queries, keys, preferred_element_type=jnp.float32) * scale
    weights = jnp.exp(scores)
    attention = weights / jnp.sum(weights, axis=-1, keepdims=True)
    low = attention.astype(jnp.bfloat16)
    attended = jnp.einsum("hst,thd->shd", low, values, preferred_element_type=jnp.float32)
    gate = jax.nn.sigmoid(logits.astype(jnp.float32))
    grad_gated = jnp.einsum(
        "sm,om->so", grad, result_map, preferred_element_type=jnp.float32
    ).reshape(rows, HEADS, head)
    grad_attended = (gate * grad_gated).astype(jnp.bfloat16)
    grad_logits = grad_gated * attended * gate * (1.0 - gate)
    grad_weights = jnp.einsum(
        "shd,thd->hst", grad_attended, values, preferred_element_type=jnp.float32
    )
    grad_scores = (
        attention
        * (grad_weights - jnp.sum(attention * grad_weights, axis=-1, keepdims=True))
        * scale
    ).astype(jnp.bfloat16)
    grad_queries = jnp.einsum("hst,thd->shd", grad_scores, keys, preferred_element_type=jnp.float32)
    grad_keys = jnp.einsum("hst,shd->thd", grad_scores, queries, preferred_element_type=jnp.float32)
    grad_values = jnp.einsum("hst,shd->thd", low, grad_attended, preferred_element_type=jnp.float32)
    grad_projected = (
        jnp.stack([grad_queries, grad_keys, grad_values, grad_logits], axis=1)
        .reshape(rows, 4 * features)
        .astype(jnp.bfloat16)
    )
    back = jnp.einsum("sa,qa->sq", grad_projected, qkvg_map, preferred_element_type=jnp.float32)
    return (grad.astype(jnp.float32) + back).astype(jnp.bfloat16)


def local(
    pair,
    first,
    second,
    incoming,
    acts,
    couple_map,
    half_map,
    qkvg_map,
    result_map,
):
    ni = lax.axis_size("ri")
    nj = lax.axis_size("rj")
    q = lax.axis_index("rj")
    rows, cols, pair_features = pair.shape
    own_rows = incoming.shape[1]
    depth = own_rows * nj
    features = incoming.shape[2]

    acts_res = lax.all_to_all(acts, "rj", split_axis=0, concat_axis=1, tiled=True)
    inc_res = lax.all_to_all(incoming, "rj", split_axis=0, concat_axis=1, tiled=True)

    left = lax.all_to_all(
        jnp.broadcast_to(first[None], (nj,) + first.shape), "rj", 0, 0, tiled=True
    ).reshape(nj, rows, own_rows, HALF)

    received = []
    for k in range(2):
        piece = lax.dynamic_slice_in_dim(second, (q + k) % 2 * cols, cols, 0)
        perm = [
            (a * nj + b, (b // 2) * nj + 2 * a + (b + k) % 2) for a in range(ni) for b in range(nj)
        ]
        received.append(lax.ppermute(piece, ("ri", "rj"), perm))
    even = q % 2 == 0
    right = jnp.stack(
        [
            jnp.where(even, received[0], received[1]),
            jnp.where(even, received[1], received[0]),
        ]
    )
    right = lax.all_to_all(
        jnp.broadcast_to(right[None], (ni,) + right.shape), "ri", 0, 0, tiled=True
    ).reshape(nj, cols, own_rows, HALF)

    outer = jnp.einsum(
        "ijk,cek->icje",
        pair,
        couple_map.reshape(HALF, HALF, pair_features),
        preferred_element_type=jnp.float32,
    ).astype(jnp.bfloat16)
    left_t = left.transpose(1, 3, 0, 2).reshape(rows, HALF, depth)
    right_t = right.transpose(1, 3, 0, 2).reshape(cols, HALF, depth)
    right_part = jnp.einsum("icje,ics->jes", outer, left_t, preferred_element_type=jnp.float32)
    right_part = (right_part / depth).astype(jnp.bfloat16)
    right_sent = lax.all_to_all(right_part, "ri", 0, 0, tiled=True)
    left_part = jnp.einsum("icje,jes->ics", outer, right_t, preferred_element_type=jnp.float32)
    left_part = (left_part / depth).astype(jnp.bfloat16)
    left_sent = lax.all_to_all(left_part, "rj", 0, 0, tiled=True)
    right_grad = jnp.sum(right_sent.astype(jnp.float32), axis=0).astype(jnp.bfloat16)
    perm = [
        (a * nj + b, (b // 2) * nj + (b % 2) * cols + a) for a in range(ni) for b in range(nj)
    ]
    right_grad = lax.ppermute(right_grad, ("ri", "rj"), perm)
    left_grad = jnp.sum(left_sent.astype(jnp.float32), axis=0).astype(jnp.bfloat16)
    factor = jnp.concatenate([left_grad, right_grad], axis=0)
    grad = (
        inc_res[0].astype(jnp.float32)
        + jnp.einsum("fs,mf->sm", factor, half_map, preferred_element_type=jnp.float32)
    ).astype(jnp.bfloat16)
    result = attention_backward(acts_res[0], grad, qkvg_map, result_map)
    return lax.all_to_all(result[None], "rj", split_axis=1, concat_axis=0, tiled=True)


def solution(mesh):
    return jax.shard_map(
        local,
        mesh=mesh,
        in_specs=(
            P("ri", "rj", None),
            P("ri", "rj"),
            P("ri", "rj"),
            P("ri", "rj", None),
            P("ri", "rj", None),
            P(),
            P(),
            P(),
            P(),
        ),
        out_specs=P("ri", "rj", None),
        check_vma=False,
    )
```

time: 564 us -> 157 us (0.28)
  blocking collectives: 328 us -> 50.3 us
  waiting for transfers between devices: 149 us -> 25.9 us
  between operations: 13.7 us -> 0.31 us
  starting transfers between devices: 45.4 us -> 55.7 us
  local copies, waits for them, and re-layouts: 17.4 us -> 8.23 us
    psum x2 -> x0, blocking collectives: 225 us -> none  [the longest x1 137 us: local(): left_total = lax.psum(left_part, 'rj')]
    psum x1 -> x0, waiting for transfers between devices: 142 us -> none  [spread(): return lax.psum(kept, axis)]
    all_gather x2 -> x0, blocking collectives: 91.6 us -> none  [the longest x1 47 us: local(): lax.all_gather(stored_second_halves, 'rj', axis=1, tiled=True)]
    all_to_all x1 -> x3, blocking collectives: 10.9 us -> 50.3 us  [the longest x1 20.2 us: local(): lax.all_to_all(result[None], 'rj', split_axis=1, concat_axis=0, tiled=True)]
    all_to_all x3 -> x4, waiting for transfers between devices: 7.09 us -> 25.1 us  [the longest x1 9 us: local(): right_sent = lax.all_to_all(right_part, 'ri', 0, 0, tiled=True)]
    ppermute x0 -> x3, starting transfers between devices: none -> 7.35 us  [the longest x1 4.45 us: local(): right_grad = lax.ppermute(right_grad, ('ri', 'rj'), perm)]
    reshape x14 -> x4, local copies, waits for them, and re-layouts: 8.23 us -> 2.38 us  [the longest x1 1.3 us: local(): left_t = left.transpose(1, 3, 0, 2).reshape(rows, HALF, depth)]
    dot_general x15 -> x12, matrix products: 9.18 us -> 14.6 us  [the longest x1 4.74 us: local(): jnp.einsum('icje,ics->jes', outer, left_t, preferred_element_type=jnp.flo...]
  transfers between devices with their start and end apart: 4 -> 7, of which waited for: 2 -> 5; matrix products, arithmetic and copies ran while one was open for 3% -> 11% of each run, Pallas kernels for 0% -> 0%
where the time goes in v1:
time: 157 us
  starting transfers between devices  55.7 us (35%)
  blocking collectives  50.3 us (32%)
  waiting for transfers between devices  25.9 us (16%)
  matrix products  14.9 us (9%)
  local copies, waits for them, and re-layouts  8.23 us (5%)
    all_to_all x1, starting transfers between devices, local(): lax.all_to_all(jnp.broadcast_to(right[None], (ni,) + right.shape), 'ri',...  25 us
    all_to_all x1, blocking collectives, local(): lax.all_to_all(result[None], 'rj', split_axis=1, concat_axis=0, tiled=True)  20.2 us
    all_to_all x1, blocking collectives, local(): lax.all_to_all(incoming, 'rj', split_axis=0, concat_axis=1, tiled=True)  18.4 us
    all_to_all x1, blocking collectives, local(): lax.all_to_all(acts, 'rj', split_axis=0, concat_axis=1, tiled=True)  11.7 us
    all_to_all x1, starting transfers between devices, local(): right_sent = lax.all_to_all(right_part, 'ri', 0, 0, tiled=True)  10.5 us
    all_to_all x1, waiting for transfers between devices, local(): right_sent = lax.all_to_all(right_part, 'ri', 0, 0, tiled=True)  9 us
    all_to_all x1, starting transfers between devices, local(): left_sent = lax.all_to_all(left_part, 'rj', 0, 0, tiled=True)  8.98 us
    all_to_all x1, waiting for transfers between devices, local(): lax.all_to_all(jnp.broadcast_to(first[None], (nj,) + first.shape), 'rj',...  6.74 us
  transfers between devices with their start and end apart: 7, of which 5 were waited for; matrix products, arithmetic and copies ran while one was open for 11% of the time, Pallas kernels for 0%

profile of v1, /device:TPU:1, one launch (start us, length us, event | category | flops | bytes accessed | tf_op | source)
XLA Modules:
  0.0 156.5 jit_solution(11325416272922613474)
XLA Ops:
  0.0 0.0 copy-start
  0.0 18.4 %all_to_all.50 = bf16[32,4,256]{2,1,0:T(4,128)(2,1)S(1)} all-to-all(bf16[32,4,256]{2,1,0:T(4,128)(2,1)} %param.12), channel_id=1, replica_groups=mesh['ri'=16,'rj'=32] {'rj'}, dimensions={0} | all-to-all | bytes 131072 | tf_op jit(solution)/shard_map/all_to_all | solution.py:70
  18.4 11.7 %all_to_all.51 = bf16[32,4,256]{2,1,0:T(4,128)(2,1)S(1)} all-to-all(bf16[32,4,256]{2,1,0:T(4,128)(2,1)} %param.13), channel_id=1, replica_groups=mesh['ri'=16,'rj'=32] {'rj'}, dimensions={0} | all-to-all | bytes 131072 | tf_op jit(solution)/shard_map/all_to_all | solution.py:69
  30.1 1.4 broadcast_in_dim.7
  31.5 3.9 %all-to-all-start.3 = ((bf16[32,32,128]{2,1,0:T(8,128)(2,1)}), bf16[32,32,128]{2,1,0:T(8,128)(2,1)S(1)}, u32[]{:S(2)}, u32[]{:S(2)}) async-start(bf16[32,32,128]{2,1,0:T(8,128)(2,1)} %broadcast_in_dim.7), calls=%async_computation.3 | async-start | bytes 524288 | tf_op jit(solution)/shard_map/all_to_all | solution.py:72
  35.5 0.7 constant_dynamic-slice_fusion.1
  36.2 0.6 collective-permute-start
  36.8 2.3 %collective-permute-start.1 = (bf16[16,128]{1,0:T(8,128)(2,1)S(1)}, bf16[16,128]{1,0:T(8,128)(2,1)S(1)}, u32[]{:S(2)}, u32[]{:S(2)}) collective-permute-start(bf16[16,128]{1,0:T(8,128)(2,1)S(1)} %get-tuple-element.8), channel_id=1, source_target_pairs={{0,1},{1,0},{2,33},{3,32},{4,65},{5,64},{6,97},{7,96},{8,129},{9,1... | collective-permute-start | bytes 12296 | tf_op jit(solution)/shard_map/ppermute | solution.py:82
  39.1 0.0 collective-permute-done
  39.1 0.8 collective-permute-done.1
  39.9 6.7 %all-to-all-done.3 = bf16[32,32,128]{2,1,0:T(8,128)(2,1)S(1)} async-done(((bf16[32,32,128]{2,1,0:T(8,128)(2,1)}), bf16[32,32,128]{2,1,0:T(8,128)(2,1)S(1)}, u32[]{:S(2)}, u32[]{:S(2)}) %all-to-all-start.3) | async-done | bytes 262176 | tf_op jit(solution)/shard_map/all_to_all | solution.py:72
  46.7 0.7 broadcast_in_dim.6
  47.3 25.0 %all-to-all-start.1 = ((bf16[16,2,16,128]{3,2,1,0:T(8,128)(2,1)}), bf16[16,2,16,128]{3,2,1,0:T(8,128)(2,1)S(1)}, u32[]{:S(2)}, u32[]{:S(2)}) async-start(bf16[16,2,16,128]{3,2,1,0:T(8,128)(2,1)} %broadcast_in_dim.6), calls=%async_computation.1 | async-start | bytes 262144 | tf_op jit(solution)/shard_map/all_to_all | solution.py:90
  72.4 4.2 %convolution_convert_fusion = bf16[32,32,32,16]{2,1,3,0:T(8,128)(2,1)} fusion(bf16[32,32,128,1]{2,1,3,0:T(8,128)(2,1)} %bitcast.143, bf16[32,16,128]{2,1,0:T(8,128)(2,1)} %param.9), kind=kOutput, calls=%fused_computation.5 | convolution fusion | flops 134742016 | bytes 1441792 | tf_op jit(solution)/shard_map/ijk,cek->icje/dot_general | solution.py:94
  76.5 0.4 reshape.48
  77.0 0.2 copy.59
  77.2 1.3 copy.71
  78.5 4.7 %fusion.25 = bf16[16,32,128]{2,1,0:T(8,128)(2,1)} fusion(bf16[32,32,128,1]{2,0,3,1:T(8,128)(2,1)S(1)} %copy.71, bf16[32,32,32,16]{2,1,3,0:T(8,128)(2,1)} %convolution_convert_fusion), kind=kOutput, calls=%fused_computation.18 | convolution fusion | flops 134348800 | bytes 1441792 | tf_op jit(solution)/shard_map/icje,ics->jes/dot_general | solution.py:102
  83.2 3.4 %all-to-all-done.1 = bf16[16,2,16,128]{3,2,1,0:T(8,128)(2,1)S(1)} async-done(((bf16[16,2,16,128]{3,2,1,0:T(8,128)(2,1)}), bf16[16,2,16,128]{3,2,1,0:T(8,128)(2,1)S(1)}, u32[]{:S(2)}, u32[]{:S(2)}) %all-to-all-start.1) | async-done | bytes 131104 | tf_op jit(solution)/shard_map/all_to_all | solution.py:90
  86.6 10.5 %all-to-all-start.4 = ((bf16[16,32,128]{2,1,0:T(8,128)(2,1)}), bf16[16,32,128]{2,1,0:T(8,128)(2,1)S(1)}, u32[]{:S(2)}, u32[]{:S(2)}) async-start(bf16[16,32,128]{2,1,0:T(8,128)(2,1)} %fusion.25), calls=%async_computation.4 | async-start | bytes 262144 | tf_op jit(solution)/shard_map/all_to_all | solution.py:104
  97.1 0.2 reshape.46
  97.4 0.1 copy.55
  97.5 0.4 copy.57
  97.9 0.0 copy-start.2
  97.9 0.0 copy-start.1
  97.9 3.5 %fusion.16 = bf16[32,32,128]{2,0,1:T(8,128)(2,1)S(1)} fusion(bf16[32,32,32,16]{2,1,3,0:T(8,128)(2,1)} %convolution_convert_fusion, bf16[16,32,128]{2,1,0:T(8,128)(2,1)S(1)} %copy.57), kind=kOutput, calls=%fused_computation.15 | convolution fusion | flops 134479872 | bytes 1441792 | tf_op jit(solution)/shard_map/icje,jes->ics/dot_general | solution.py:105
  101.4 0.8 copy.58
  102.2 9.0 %all-to-all-done.4 = bf16[16,32,128]{2,1,0:T(8,128)(2,1)S(1)} async-done(((bf16[16,32,128]{2,1,0:T(8,128)(2,1)}), bf16[16,32,128]{2,1,0:T(8,128)(2,1)S(1)}, u32[]{:S(2)}, u32[]{:S(2)}) %all-to-all-start.4) | async-done | bytes 131104 | tf_op jit(solution)/shard_map/all_to_all | solution.py:104
  111.2 9.0 %all-to-all-start.2 = ((bf16[32,32,128]{2,1,0:T(8,128)(2,1)}), bf16[32,32,128]{2,1,0:T(8,128)(2,1)S(1)}, u32[]{:S(2)}, u32[]{:S(2)}) async-start(bf16[32,32,128]{2,1,0:T(8,128)(2,1)} %copy.58), calls=%async_computation.2 | async-start | bytes 524288 | tf_op jit(solution)/shard_map/all_to_all | solution.py:107
  120.2 0.0 copy-done
  120.2 0.2 convolution_convert_fusion.1
  120.5 0.2 copy.61
  120.7 4.4 %collective-permute-start.2 = (bf16[32,128]{1,0:T(8,128)(2,1)S(1)}, bf16[32,128]{1,0:T(8,128)(2,1)S(1)}, u32[]{:S(2)}, u32[]{:S(2)}) collective-permute-start(bf16[32,128]{1,0:T(8,128)(2,1)S(1)} %reduce_sum.43), channel_id=1, source_target_pairs={{0,0},{1,16},{2,32},{3,48},{4,64},{5,80},{6,96},{7,112},{8,128},{9... | collective-permute-start | bytes 24584 | tf_op jit(solution)/shard_map/ppermute | solution.py:112
  125.1 0.3 fusion.44
  125.5 6.0 %all-to-all-done.2 = bf16[32,32,128]{2,1,0:T(8,128)(2,1)S(1)} async-done(((bf16[32,32,128]{2,1,0:T(8,128)(2,1)}), bf16[32,32,128]{2,1,0:T(8,128)(2,1)S(1)}, u32[]{:S(2)}, u32[]{:S(2)}) %all-to-all-start.2) | async-done | bytes 262176 | tf_op jit(solution)/shard_map/all_to_all | solution.py:107
  131.5 0.1 reduce_sum.42
  131.5 0.0 collective-permute-done.2
  131.5 0.0 copy-done.2
  131.5 0.2 fusion.33
  131.7 0.0 copy-done.1
  131.7 0.2 fusion.66
  131.9 0.2 fusion.38
  132.1 0.2 fusion.36
  132.3 0.3 fusion.53
  132.7 0.3 fusion.35
  132.9 0.3 fusion.34
  133.2 0.3 fusion.37
  133.6 0.1 copy.85
  133.7 0.5 broadcast.45
  134.2 1.0 reduce.4
  135.3 20.2 %all_to_all.52 = bf16[32,2,512]{2,1,0:T(2,128)(2,1)S(1)} all-to-all(bf16[32,2,512]{2,1,0:T(2,128)(2,1)S(1)} %reshape.62), channel_id=1, replica_groups=mesh['ri'=16,'rj'=32] {'rj'}, dimensions={0} | all-to-all | bytes 131072 | tf_op jit(solution)/shard_map/all_to_all | solution.py:120
  155.5 0.1 reshape.63
  155.5 0.4 bitcast_reduce_fusion
  155.9 0.7 all_to_all.42
  (7 shorter events, 0.2 us)
Async XLA Ops:
  0.0 120.2 %copy-start = (bf16[256,1024]{1,0:T(8,128)(2,1)S(1)}, bf16[256,1024]{1,0:T(8,128)(2,1)}, u32[]{:S(2)}) copy-start(bf16[256,1024]{1,0:T(8,128)(2,1)} %param.16) | copy-start | bytes 1572868
  31.5 15.1 %all-to-all-start.3 = ((bf16[32,32,128]{2,1,0:T(8,128)(2,1)}), bf16[32,32,128]{2,1,0:T(8,128)(2,1)S(1)}, u32[]{:S(2)}, u32[]{:S(2)}) async-start(bf16[32,32,128]{2,1,0:T(8,128)(2,1)} %broadcast_in_dim.7), calls=%async_computation.3 | async-start | bytes 524288 | tf_op jit(solution)/shard_map/all_to_all | solution.py:72
  36.2 2.9 %collective-permute-start = (bf16[16,128]{1,0:T(8,128)(2,1)S(1)}, bf16[16,128]{1,0:T(8,128)(2,1)S(1)}, u32[]{:S(2)}, u32[]{:S(2)}) collective-permute-start(bf16[16,128]{1,0:T(8,128)(2,1)S(1)} %get-tuple-element.7), channel_id=1, source_target_pairs={{0,0},{1,1},{2,32},{3,33},{4,64},{5,65},{6,96},{7,97},{8,128},{9,1... | collective-permute-start | bytes 12296 | tf_op jit(solution)/shard_map/ppermute | solution.py:82
  36.8 3.1 %collective-permute-start.1 = (bf16[16,128]{1,0:T(8,128)(2,1)S(1)}, bf16[16,128]{1,0:T(8,128)(2,1)S(1)}, u32[]{:S(2)}, u32[]{:S(2)}) collective-permute-start(bf16[16,128]{1,0:T(8,128)(2,1)S(1)} %get-tuple-element.8), channel_id=1, source_target_pairs={{0,1},{1,0},{2,33},{3,32},{4,65},{5,64},{6,97},{7,96},{8,129},{9,1... | collective-permute-start | bytes 12296 | tf_op jit(solution)/shard_map/ppermute | solution.py:82
  47.3 39.3 %all-to-all-start.1 = ((bf16[16,2,16,128]{3,2,1,0:T(8,128)(2,1)}), bf16[16,2,16,128]{3,2,1,0:T(8,128)(2,1)S(1)}, u32[]{:S(2)}, u32[]{:S(2)}) async-start(bf16[16,2,16,128]{3,2,1,0:T(8,128)(2,1)} %broadcast_in_dim.6), calls=%async_computation.1 | async-start | bytes 262144 | tf_op jit(solution)/shard_map/all_to_all | solution.py:90
  86.6 24.6 %all-to-all-start.4 = ((bf16[16,32,128]{2,1,0:T(8,128)(2,1)}), bf16[16,32,128]{2,1,0:T(8,128)(2,1)S(1)}, u32[]{:S(2)}, u32[]{:S(2)}) async-start(bf16[16,32,128]{2,1,0:T(8,128)(2,1)} %fusion.25), calls=%async_computation.4 | async-start | bytes 262144 | tf_op jit(solution)/shard_map/all_to_all | solution.py:104
  97.9 33.6 %copy-start.2 = (bf16[256,64]{0,1:T(8,128)(2,1)S(1)}, bf16[256,64]{0,1:T(8,128)(2,1)}, u32[]{:S(2)}) copy-start(bf16[256,64]{0,1:T(8,128)(2,1)} %param.15) | copy-start | bytes 98308
  97.9 33.8 %copy-start.1 = (bf16[256,256]{1,0:T(8,128)(2,1)S(1)}, bf16[256,256]{1,0:T(8,128)(2,1)}, u32[]{:S(2)}) copy-start(bf16[256,256]{1,0:T(8,128)(2,1)} %param.17) | copy-start | bytes 393220
  111.2 20.3 %all-to-all-start.2 = ((bf16[32,32,128]{2,1,0:T(8,128)(2,1)}), bf16[32,32,128]{2,1,0:T(8,128)(2,1)S(1)}, u32[]{:S(2)}, u32[]{:S(2)}) async-start(bf16[32,32,128]{2,1,0:T(8,128)(2,1)} %copy.58), calls=%async_computation.2 | async-start | bytes 524288 | tf_op jit(solution)/shard_map/all_to_all | solution.py:107
  120.7 10.8 %collective-permute-start.2 = (bf16[32,128]{1,0:T(8,128)(2,1)S(1)}, bf16[32,128]{1,0:T(8,128)(2,1)S(1)}, u32[]{:S(2)}, u32[]{:S(2)}) collective-permute-start(bf16[32,128]{1,0:T(8,128)(2,1)S(1)} %reduce_sum.43), channel_id=1, source_target_pairs={{0,0},{1,16},{2,32},{3,48},{4,64},{5,80},{6,96},{7,112},{8,128},{9... | collective-permute-start | bytes 24584 | tf_op jit(solution)/shard_map/ppermute | solution.py:112

commit v2 on v1

--- a/solution.py
+++ b/solution.py
@@ -60,64 +60,82 @@
 ):
     ni = lax.axis_size("ri")
     nj = lax.axis_size("rj")
-    q = lax.axis_index("rj")
+    chips = nj // 2
+    core = lax.axis_index("rj") % 2
     rows, cols, pair_features = pair.shape
     own_rows = incoming.shape[1]
     depth = own_rows * nj
+    share = depth // 2
     features = incoming.shape[2]
+    both = ("ri", "rj")
 
-    acts_res = lax.all_to_all(acts, "rj", split_axis=0, concat_axis=1, tiled=True)
-    inc_res = lax.all_to_all(incoming, "rj", split_axis=0, concat_axis=1, tiled=True)
+    other = lax.ppermute(pair, both, [(n, n ^ 1) for n in range(ni * nj)])
+    is_even = core == 0
+    chip_pair = jnp.stack(
+        [jnp.where(is_even, pair, other), jnp.where(is_even, other, pair)], axis=1
+    )
 
-    left = lax.all_to_all(
-        jnp.broadcast_to(first[None], (nj,) + first.shape), "rj", 0, 0, tiled=True
-    ).reshape(nj, rows, own_rows, HALF)
-
-    received = []
-    for k in range(2):
-        piece = lax.dynamic_slice_in_dim(second, (q + k) % 2 * cols, cols, 0)
-        perm = [
-            (a * nj + b, (b // 2) * nj + 2 * a + (b + k) % 2) for a in range(ni) for b in range(nj)
-        ]
-        received.append(lax.ppermute(piece, ("ri", "rj"), perm))
-    even = q % 2 == 0
-    right = jnp.stack(
-        [
-            jnp.where(even, received[0], received[1]),
-            jnp.where(even, received[1], received[0]),
-        ]
+    halves = jnp.concatenate([first, second], axis=0)
+    groups = [[2 * m + c for m in range(chips)] for c in range(2)]
+    gathered = lax.all_to_all(
+        jnp.broadcast_to(halves[None], (chips,) + halves.shape),
+        "rj",
+        0,
+        0,
+        axis_index_groups=groups,
+        tiled=True,
     )
-    right = lax.all_to_all(
-        jnp.broadcast_to(right[None], (ni,) + right.shape), "ri", 0, 0, tiled=True
-    ).reshape(nj, cols, own_rows, HALF)
+    left = gathered[:, :rows].reshape(chips, rows, own_rows, HALF)
 
     outer = jnp.einsum(
-        "ijk,cek->icje",
-        pair,
+        "injk,cek->icnje",
+        chip_pair,
         couple_map.reshape(HALF, HALF, pair_features),
         preferred_element_type=jnp.float32,
-    ).astype(jnp.bfloat16)
-    left_t = left.transpose(1, 3, 0, 2).reshape(rows, HALF, depth)
-    right_t = right.transpose(1, 3, 0, 2).reshape(cols, HALF, depth)
+    ).astype(jnp.bfloat16).reshape(rows, HALF, 2 * cols, HALF)
+    left_t = left.transpose(1, 3, 0, 2).reshape(rows, HALF, share)
     right_part = jnp.einsum("icje,ics->jes", outer, left_t, preferred_element_type=jnp.float32)
     right_part = (right_part / depth).astype(jnp.bfloat16)
-    right_sent = lax.all_to_all(right_part, "ri", 0, 0, tiled=True)
+    right_part = right_part.reshape(2, cols * HALF, share)
+    right_part = jnp.concatenate([right_part[0], right_part[1]], axis=1)
+    moved = jnp.concatenate([gathered[:, rows:].reshape(chips * rows, 128), right_part], axis=0)
+    swap = [
+        (p * nj + 2 * m + c, m * nj + 2 * p + c)
+        for p in range(ni)
+        for m in range(chips)
+        for c in range(2)
+    ]
+    moved = lax.ppermute(moved, both, swap)
+
+    (acts, incoming), _ = lax.optimization_barrier(((acts, incoming), right_part))
+    attn_in = lax.all_to_all(
+        jnp.concatenate([acts, incoming], axis=1), "rj", 0, 0, tiled=True
+    )
+    acts_res = attn_in[:, :own_rows].reshape(depth, features)
+    inc_res = attn_in[:, own_rows:].reshape(depth, features)
+
+    right = moved[: chips * rows].reshape(chips, 2 * cols, own_rows, HALF)
+    right_t = right.transpose(1, 3, 0, 2).reshape(2 * cols, HALF, share)
     left_part = jnp.einsum("icje,jes->ics", outer, right_t, preferred_element_type=jnp.float32)
     left_part = (left_part / depth).astype(jnp.bfloat16)
-    left_sent = lax.all_to_all(left_part, "rj", 0, 0, tiled=True)
-    right_grad = jnp.sum(right_sent.astype(jnp.float32), axis=0).astype(jnp.bfloat16)
-    perm = [
-        (a * nj + b, (b // 2) * nj + (b % 2) * cols + a) for a in range(ni) for b in range(nj)
-    ]
-    right_grad = lax.ppermute(right_grad, ("ri", "rj"), perm)
-    left_grad = jnp.sum(left_sent.astype(jnp.float32), axis=0).astype(jnp.bfloat16)
-    factor = jnp.concatenate([left_grad, right_grad], axis=0)
+    right_back = moved[chips * rows :]
+    right_back = jnp.concatenate([right_back[:, :share], right_back[:, share:]], axis=0)
+    sums = jnp.concatenate([left_part, right_back.reshape(rows, HALF, share)], axis=2)
+    sums = lax.all_to_all(sums, "rj", 0, 0, tiled=True)
+    sums = jnp.sum(
+        sums.reshape(chips, 2, HALF, 2, share).astype(jnp.float32), axis=0
+    ).astype(jnp.bfloat16)
+    factor = (
+        sums.reshape(2, HALF, 2, chips, own_rows)
+        .transpose(2, 1, 3, 0, 4)
+        .reshape(2 * HALF, depth)
+    )
     grad = (
-        inc_res[0].astype(jnp.float32)
+        inc_res.astype(jnp.float32)
         + jnp.einsum("fs,mf->sm", factor, half_map, preferred_element_type=jnp.float32)
     ).astype(jnp.bfloat16)
-    result = attention_backward(acts_res[0], grad, qkvg_map, result_map)
-    return lax.all_to_all(result[None], "rj", split_axis=1, concat_axis=0, tiled=True)
+    result = attention_backward(acts_res, grad, qkvg_map, result_map)
+    return lax.all_to_all(result.reshape(nj, own_rows, features), "rj", 0, 0, tiled=True)
 
 
 def solution(mesh):

time: 157 us -> 122 us (0.78); the launches traced: 157 us -> 120 us
  blocking collectives: 50.3 us -> 11.4 us
  local copies, waits for them, and re-layouts: 8.23 us -> 28.9 us
  starting transfers between devices: 55.7 us -> 40 us
  waiting for transfers between devices: 25.9 us -> 11.4 us
  matrix products: 14.9 us -> 23.6 us
  other arithmetic: 1.15 us -> 4.14 us
    all_to_all x3 -> x1, blocking collectives: 50.3 us -> 11.4 us  [local(): lax.all_to_all(result.reshape(nj, own_rows, features), 'rj', 0, 0, tiled=...]
    reshape x4 -> x9, local copies, waits for them, and re-layouts: 2.38 us -> 17.8 us  [the longest x1 15.3 us: local(): outer = jnp.einsum('injk,cek->icnje', chip_pair, couple_map.reshape(HALF,...]
    all_to_all x4 -> x3, waiting for transfers between devices: 25.1 us -> 10.2 us  [the longest x1 10.2 us: local(): sums = lax.all_to_all(sums, 'rj', 0, 0, tiled=True)]
    all_to_all x4 -> x3, starting transfers between devices: 48.4 us -> 36.2 us  [the longest x1 19.3 us: local(): lax.all_to_all(jnp.concatenate([acts, incoming], axis=1), 'rj', 0, 0, til...]
    convert_element_type x2, local copies, waits for them, and re-layouts: 0.82 us -> 8.37 us  [the longest x1 8.33 us: local(): outer = jnp.einsum('injk,cek->icnje', chip_pair, couple_map.reshape(HALF,...]
    dot_general x1, matrix products: 4.74 us -> 9.47 us  [local(): jnp.einsum('icje,ics->jes', outer, left_t, preferred_element_type=jnp.flo...]
    ppermute x3 -> x2, starting transfers between devices: 7.35 us -> 3.81 us  [the longest x1 3.13 us: local(): other = lax.ppermute(pair, both, [(n, n ^ 1) for n in range(ni * nj)])]
    concatenate x0 -> x5, other arithmetic: none -> 2.52 us  [the longest x1 0.85 us: local(): jnp.concatenate([left_part, right_back.reshape(rows, HALF, share)], axis=2)]
  transfers between devices with their start and end apart: 7 -> 5, of which waited for: 5 -> 2; matrix products, arithmetic and copies ran while one was open for 11% -> 34% of each run, Pallas kernels for 0% -> 0%
where the time goes in v2:
time: 122 us; the launch traced here: 120 us
  starting transfers between devices  40 us (33%)
  local copies, waits for them, and re-layouts  28.9 us (24%)
  matrix products  23.6 us (19%)
  waiting for transfers between devices  11.4 us (9%)
  blocking collectives  11.4 us (9%)
  other arithmetic  4.14 us (3%)
    all_to_all x1, starting transfers between devices, local(): lax.all_to_all(jnp.concatenate([acts, incoming], axis=1), 'rj', 0, 0, til...  19.3 us
    reshape x1, local copies, waits for them, and re-layouts, local(): outer = jnp.einsum('injk,cek->icnje', chip_pair, couple_map.reshape(HALF,...  15.3 us
    all_to_all x1, blocking collectives, local(): lax.all_to_all(result.reshape(nj, own_rows, features), 'rj', 0, 0, tiled=...  11.4 us
    all_to_all x1, waiting for transfers between devices, local(): sums = lax.all_to_all(sums, 'rj', 0, 0, tiled=True)  10.2 us
    dot_general x1, matrix products, local(): jnp.einsum('icje,ics->jes', outer, left_t, preferred_element_type=jnp.flo...  9.47 us
    all_to_all x1, starting transfers between devices, local(): lax.all_to_all(jnp.broadcast_to(halves[None], (chips,) + halves.shape), '...  9.19 us
    convert_element_type x1, local copies, waits for them, and re-layouts, local(): outer = jnp.einsum('injk,cek->icnje', chip_pair, couple_map.reshape(HALF,...  8.33 us
    all_to_all x1, starting transfers between devices, local(): sums = lax.all_to_all(sums, 'rj', 0, 0, tiled=True)  7.73 us
  transfers between devices with their start and end apart: 5, of which 2 were waited for; matrix products, arithmetic and copies ran while one was open for 34% of the time, Pallas kernels for 0%

profile of v2, /device:TPU:1, one launch (start us, length us, event | category | flops | bytes accessed | tf_op | source)
XLA Modules:
  0.0 119.7 jit_solution(746385346912510139)
XLA Ops:
  0.0 0.0 copy-start
  0.0 0.8 pad_maximum_fusion.4
  0.8 0.8 broadcast_in_dim.2
  1.5 9.2 %all-to-all-start = ((bf16[16,64,128]{2,1,0:T(8,128)(2,1)}), bf16[16,64,128]{2,1,0:T(8,128)(2,1)S(1)}, u32[]{:S(2)}, u32[]{:S(2)}) async-start(bf16[16,64,128]{2,1,0:T(8,128)(2,1)} %broadcast_in_dim.2), calls=%async_computation | async-start | bytes 524288 | tf_op jit(solution)/shard_map/all_to_all | solution.py:80
  10.7 3.1 %collective-permute-start = (bf16[32,16,128]{2,1,0:T(8,128)(2,1)}, bf16[32,16,128]{2,1,0:T(8,128)(2,1)S(1)}, u32[]{:S(2)}, u32[]{:S(2)}) collective-permute-start(bf16[32,16,128]{2,1,0:T(8,128)(2,1)} %param.9), channel_id=1, source_target_pairs={{0,1},{1,0},{2,3},{3,2},{4,5},{5,4},{6,7},{7,6},{8,9},{9,8},{10,11... | collective-permute-start | bytes 393224 | tf_op jit(solution)/shard_map/ppermute | solution.py:72
  13.9 1.2 collective-permute-done
  15.0 0.9 select_bitcast_fusion.1
  16.0 6.5 %convert_bitcast_fusion = bf16[32,32,2,16,32]{4,3,1,2,0:T(8,128)(2,1)} fusion(bf16[32,32,128,1,1]{2,1,0,4,3:T(8,128)(2,1)} %bitcast.143, bf16[32,1,16,128]{3,2,1,0:T(8,128)(2,1)S(1)} %get-tuple-element.16, bf16[32,1,16,128]{3,2,1,0:T(8,128)(2,1)S(1)} %get-tuple-element.15), kind=kOutput, calls=%fused_computation.3 | convolution fusion | flops 270008320 | bytes 2621440 | tf_op jit(solution)/shard_map/injk,cek->icnje/dot_general | solution.py:90
  22.5 8.3 %copy.73 = bf16[32,32,2,16,32]{4,3,2,1,0:T(8,128)(2,1)} copy(bf16[32,32,2,16,32]{4,3,1,2,0:T(8,128)(2,1)} %convert_bitcast_fusion) | data formatting | bytes 4194304 | tf_op jit(solution)/shard_map/convert_element_type | solution.py:95
  30.8 0.0 all-to-all-done
  30.9 0.2 reshape.65
  31.1 0.1 copy.74
  31.2 0.8 copy.76
  32.0 0.0 copy-start.2
  32.0 0.0 copy-start.3
  32.0 9.5 %fusion.14 = bf16[32,32,64]{2,1,0:T(8,128)(2,1)S(1)} fusion(bf16[32,32,32,32]{3,2,1,0:T(8,128)(2,1)} %bitcast.123, bf16[32,32,64]{2,0,1:T(8,128)(2,1)S(1)} %copy.76), kind=kOutput, calls=%fused_computation.13 | convolution fusion | flops 134348800 | bytes 2359296 | tf_op jit(solution)/shard_map/icje,ics->jes/dot_general | solution.py:97
  41.5 0.1 maximum_maximum_fusion
  41.7 0.7 collective-permute-start.1
  42.3 0.0 copy-done.2
  42.3 0.0 copy-done.3
  42.4 0.7 pad_maximum_fusion.3
  43.1 19.3 %all-to-all-start.1 = ((bf16[32,8,256]{2,1,0:T(8,128)(2,1)}), bf16[32,8,256]{2,1,0:T(8,128)(2,1)S(1)}, u32[]{:S(2)}, u32[]{:S(2)}) async-start(bf16[32,8,256]{2,1,0:T(8,128)(2,1)} %pad_maximum_fusion.3), calls=%async_computation.1 | async-start | bytes 262144 | tf_op jit(solution)/shard_map/all_to_all | solution.py:111
  62.4 15.3 %copy.79 = bf16[32,32,32,32]{2,1,3,0:T(8,128)(2,1)} copy(bf16[32,32,32,32]{3,2,1,0:T(8,128)(2,1)} %bitcast.124) | data formatting | bytes 4194304 | tf_op jit(solution)/shard_map/reshape | solution.py:95
  77.7 0.0 collective-permute-done.1
  77.8 0.1 copy.77
  77.9 0.3 reshape.68
  78.2 0.6 copy.78
  78.7 0.8 copy.80
  79.5 0.1 fusion.54
  79.6 0.1 pad_maximum_fusion
  79.7 0.0 copy-start.4
  79.7 0.0 copy-start.1
  79.7 5.1 %fusion.18 = bf16[32,32,64]{2,1,0:T(8,128)(2,1)S(1)} fusion(bf16[32,32,32,32]{2,1,3,0:T(8,128)(2,1)} %copy.79, bf16[32,32,64]{2,0,1:T(8,128)(2,1)S(1)} %copy.80), kind=kOutput, calls=%fused_computation.15 | convolution fusion | flops 134348800 | bytes 2359296 | tf_op jit(solution)/shard_map/icje,jes->ics/dot_general | solution.py:119
  84.8 0.9 pad_maximum_fusion.1
  85.7 0.0 all-to-all-done.1
  85.7 7.7 %all-to-all-start.2 = ((bf16[32,32,128]{2,1,0:T(8,128)(2,1)}), bf16[32,32,128]{2,1,0:T(8,128)(2,1)S(1)}, u32[]{:S(2)}, u32[]{:S(2)}) async-start(bf16[32,32,128]{2,1,0:T(8,128)(2,1)} %pad_maximum_fusion.1), calls=%async_computation.2 | async-start | bytes 524288 | tf_op jit(solution)/shard_map/all_to_all | solution.py:124
  93.6 0.0 copy-done
  93.6 0.2 convolution_convert_fusion
  93.8 0.2 copy.83
  94.0 0.3 fusion.38
  94.3 10.2 %all-to-all-done.2 = bf16[32,32,128]{2,1,0:T(8,128)(2,1)S(1)} async-done(((bf16[32,32,128]{2,1,0:T(8,128)(2,1)}), bf16[32,32,128]{2,1,0:T(8,128)(2,1)S(1)}, u32[]{:S(2)}, u32[]{:S(2)}) %all-to-all-start.2) | async-done | bytes 262176 | tf_op jit(solution)/shard_map/all_to_all | solution.py:124
  104.5 0.2 reshape.71
  104.8 0.6 reduce_sum.30
  105.4 0.1 copy.81
  105.5 0.1 copy.82
  105.6 0.1 reshape.73
  105.7 0.0 copy-done.4
  105.7 0.1 fusion.24
  105.8 0.0 copy-done.1
  105.8 0.2 fusion.58
  106.0 0.2 fusion.28
  106.2 0.2 fusion.27
  106.5 0.3 fusion.44
  106.8 0.3 fusion.26
  107.0 0.3 fusion.25
  107.4 0.3 fusion.23
  107.7 11.4 %all_to_all.20 = bf16[32,4,256]{2,1,0:T(4,128)(2,1)S(1)} all-to-all(bf16[32,4,256]{2,1,0:T(4,128)(2,1)S(1)} %reshape.77), channel_id=1, replica_groups=mesh['ri'=16,'rj'=32] {'rj'}, dimensions={0} | all-to-all | bytes 131072 | tf_op jit(solution)/shard_map/all_to_all | solution.py:138
  119.1 0.6 copy.107
  (8 shorter events, 0.2 us)
Async XLA Ops:
  0.0 93.6 %copy-start = (bf16[256,1024]{1,0:T(8,128)(2,1)S(1)}, bf16[256,1024]{1,0:T(8,128)(2,1)}, u32[]{:S(2)}) copy-start(bf16[256,1024]{1,0:T(8,128)(2,1)} %param.16) | copy-start | bytes 1572868
  1.5 29.3 %all-to-all-start = ((bf16[16,64,128]{2,1,0:T(8,128)(2,1)}), bf16[16,64,128]{2,1,0:T(8,128)(2,1)S(1)}, u32[]{:S(2)}, u32[]{:S(2)}) async-start(bf16[16,64,128]{2,1,0:T(8,128)(2,1)} %broadcast_in_dim.2), calls=%async_computation | async-start | bytes 524288 | tf_op jit(solution)/shard_map/all_to_all | solution.py:80
  10.7 4.3 %collective-permute-start = (bf16[32,16,128]{2,1,0:T(8,128)(2,1)}, bf16[32,16,128]{2,1,0:T(8,128)(2,1)S(1)}, u32[]{:S(2)}, u32[]{:S(2)}) collective-permute-start(bf16[32,16,128]{2,1,0:T(8,128)(2,1)} %param.9), channel_id=1, source_target_pairs={{0,1},{1,0},{2,3},{3,2},{4,5},{5,4},{6,7},{7,6},{8,9},{9,8},{10,11... | collective-permute-start | bytes 393224 | tf_op jit(solution)/shard_map/ppermute | solution.py:72
  32.0 10.3 %copy-start.2 = (bf16[32,4,256]{2,1,0:T(4,128)(2,1)S(1)}, bf16[32,4,256]{2,1,0:T(4,128)(2,1)}, u32[]{:S(2)}) copy-start(bf16[32,4,256]{2,1,0:T(4,128)(2,1)} %param.12) | copy-start | bytes 196612
  32.0 10.3 %copy-start.3 = (bf16[32,4,256]{2,1,0:T(4,128)(2,1)S(1)}, bf16[32,4,256]{2,1,0:T(4,128)(2,1)}, u32[]{:S(2)}) copy-start(bf16[32,4,256]{2,1,0:T(4,128)(2,1)} %param.13) | copy-start | bytes 196612
  41.7 36.1 %collective-permute-start.1 = (bf16[1024,128]{1,0:T(8,128)(2,1)S(1)}, bf16[1024,128]{1,0:T(8,128)(2,1)S(1)}, u32[]{:S(2)}, u32[]{:S(2)}) collective-permute-start(bf16[1024,128]{1,0:T(8,128)(2,1)S(1)} %maximum_maximum_fusion), channel_id=1, source_target_pairs={{0,0},{1,1},{2,32},{3,33},{4,64},{5,65},{6,96},{7,97},{8,128},{9,1... | collective-permute-start | bytes 786440 | tf_op jit(solution)/shard_map/ppermute | solution.py:108
  43.1 42.6 %all-to-all-start.1 = ((bf16[32,8,256]{2,1,0:T(8,128)(2,1)}), bf16[32,8,256]{2,1,0:T(8,128)(2,1)S(1)}, u32[]{:S(2)}, u32[]{:S(2)}) async-start(bf16[32,8,256]{2,1,0:T(8,128)(2,1)} %pad_maximum_fusion.3), calls=%async_computation.1 | async-start | bytes 262144 | tf_op jit(solution)/shard_map/all_to_all | solution.py:111
  79.7 26.0 %copy-start.4 = (bf16[256,64]{0,1:T(8,128)(2,1)S(1)}, bf16[256,64]{0,1:T(8,128)(2,1)}, u32[]{:S(2)}) copy-start(bf16[256,64]{0,1:T(8,128)(2,1)} %param.15) | copy-start | bytes 98308
  79.7 26.1 %copy-start.1 = (bf16[256,256]{1,0:T(8,128)(2,1)S(1)}, bf16[256,256]{1,0:T(8,128)(2,1)}, u32[]{:S(2)}) copy-start(bf16[256,256]{1,0:T(8,128)(2,1)} %param.17) | copy-start | bytes 393220
  85.7 18.8 %all-to-all-start.2 = ((bf16[32,32,128]{2,1,0:T(8,128)(2,1)}), bf16[32,32,128]{2,1,0:T(8,128)(2,1)S(1)}, u32[]{:S(2)}, u32[]{:S(2)}) async-start(bf16[32,32,128]{2,1,0:T(8,128)(2,1)} %pad_maximum_fusion.1), calls=%async_computation.2 | async-start | bytes 524288 | tf_op jit(solution)/shard_map/all_to_all | solution.py:124

commit v3 on v2

--- a/solution.py
+++ b/solution.py
@@ -1,10 +1,18 @@
+import functools
+
 import jax
 import jax.numpy as jnp
 from jax import lax
+from jax.experimental import pallas as pl
+from jax.experimental.pallas import tpu as pltpu
 from jax.sharding import PartitionSpec as P
 
 HALF = 32
 HEADS = 8
+NT = (((1,), (1,)), ((), ()))
+VMEM = pl.BlockSpec(memory_space=pltpu.VMEM)
+SMEM = pl.BlockSpec(memory_space=pltpu.SMEM)
+LIMIT = 40 * 1024 * 1024
 
 
 def attention_backward(acts, grad, qkvg_map, result_map):
@@ -45,6 +53,99 @@
     )
     back = jnp.einsum("sa,qa->sq", grad_projected, qkvg_map, preferred_element_type=jnp.float32)
     return (grad.astype(jnp.float32) + back).astype(jnp.bfloat16)
+
+
+def outer_blocks(lhs, pieces, store):
+    count = pieces[0].shape[0]
+    zero = jnp.zeros((HALF, 128), jnp.bfloat16)
+    for n in range(count):
+        stacked = []
+        for piece in pieces:
+            x = piece[n]
+            for g in range(4):
+                stacked.append(
+                    jnp.concatenate([x if h == g else zero for h in range(4)], axis=1)
+                )
+        product = lax.dot_general(
+            lhs, jnp.concatenate(stacked, axis=0), NT, preferred_element_type=jnp.float32
+        ).astype(jnp.bfloat16)
+        for m in range(len(pieces)):
+            for g in range(8):
+                store(
+                    m, n, g, product[g * HALF : (g + 1) * HALF, m * 128 : (m + 1) * 128]
+                )
+
+
+def outer_right_kernel(core_ref, lhs_ref, own_ref, other_ref, out_ref):
+    cols = own_ref.shape[0]
+    core = core_ref[0]
+    starts = [core * (cols * HALF), (1 - core) * (cols * HALF)]
+
+    def store(m, n, g, block):
+        row = pl.multiple_of(starts[m] + n * HALF, HALF)
+        out_ref[pl.ds(row, HALF), g * 128 : (g + 1) * 128] = block
+
+    outer_blocks(lhs_ref[...], [own_ref, other_ref], store)
+
+
+def outer_left_kernel(lhs_ref, pair_ref, out_ref):
+    half = pair_ref.shape[0] // 2
+
+    def store(m, n, g, block):
+        row = (m * half + n) * HALF
+        out_ref[row : row + HALF, g * 128 : (g + 1) * 128] = block
+
+    outer_blocks(lhs_ref[...], [pair_ref.at[:half], pair_ref.at[half:]], store)
+
+
+def right_kernel(scale, outer_ref, gathered_ref, out_ref):
+    to = lax.broadcasted_iota(jnp.int32, (128, 128), 0)
+    at = lax.broadcasted_iota(jnp.int32, (128, 128), 1)
+    want = ((to & 63) >> 2) * 8 + (to >> 6) * 4 + (to & 3)
+    order = jnp.where(at == want, 1.0, 0.0).astype(jnp.bfloat16)
+    sorted_rows = jnp.dot(
+        order, gathered_ref[...], preferred_element_type=jnp.float32
+    ).astype(jnp.bfloat16)
+    left = sorted_rows[:64]
+    none = jnp.zeros_like(left)
+    low = lax.dot_general(
+        outer_ref[:512], jnp.concatenate([left, none], axis=0), NT,
+        preferred_element_type=jnp.float32,
+    )
+    high = lax.dot_general(
+        outer_ref[512:], jnp.concatenate([none, left], axis=0), NT,
+        preferred_element_type=jnp.float32,
+    )
+    out_ref[:512] = ((low + high) * scale).astype(jnp.bfloat16)
+    for block in range(8):
+        out_ref[512 + block * 64 : 576 + block * 64] = sorted_rows[
+            64:, block * 128 : (block + 1) * 128
+        ]
+
+
+def left_kernel(scale, outer_ref, moved_ref, out_ref):
+    right = jnp.concatenate(
+        [moved_ref[512 + block * 64 : 576 + block * 64] for block in range(8)], axis=1
+    )
+    sums = lax.dot_general(
+        outer_ref[...], jnp.concatenate([right, jnp.zeros_like(right)], axis=0), NT,
+        preferred_element_type=jnp.float32,
+    ) * scale
+    packed = moved_ref[:512].astype(jnp.float32)
+    is_left = lax.broadcasted_iota(jnp.int32, (512, 128), 1) < 64
+    out_ref[:512] = jnp.where(is_left, sums[:512], pltpu.roll(packed, 64, 1)).astype(jnp.bfloat16)
+    out_ref[512:] = jnp.where(is_left, sums[512:], packed).astype(jnp.bfloat16)
+
+
+def call(kernel, shape, specs, flops):
+    return pl.pallas_call(
+        kernel,
+        out_shape=jax.ShapeDtypeStruct(shape, jnp.bfloat16),
+        in_specs=specs,
+        out_specs=VMEM,
+        compiler_params=pltpu.CompilerParams(vmem_limit_bytes=LIMIT),
+        cost_estimate=pl.CostEstimate(flops=flops, bytes_accessed=4 << 20, transcendentals=0),
+    )
 
 
 def local(
@@ -68,14 +169,10 @@
     share = depth // 2
     features = incoming.shape[2]
     both = ("ri", "rj")
-
-    other = lax.ppermute(pair, both, [(n, n ^ 1) for n in range(ni * nj)])
-    is_even = core == 0
-    chip_pair = jnp.stack(
-        [jnp.where(is_even, pair, other), jnp.where(is_even, other, pair)], axis=1
-    )
-
-    halves = jnp.concatenate([first, second], axis=0)
+    wide = rows * HALF
+
+    halves = jnp.stack([first, second]).reshape(2, rows, own_rows, HALF)
+    halves = halves.transpose(0, 2, 3, 1).reshape(2 * own_rows, wide)
     groups = [[2 * m + c for m in range(chips)] for c in range(2)]
     gathered = lax.all_to_all(
         jnp.broadcast_to(halves[None], (chips,) + halves.shape),
@@ -84,44 +181,50 @@
         0,
         axis_index_groups=groups,
         tiled=True,
-    )
-    left = gathered[:, :rows].reshape(chips, rows, own_rows, HALF)
-
-    outer = jnp.einsum(
-        "injk,cek->icnje",
-        chip_pair,
-        couple_map.reshape(HALF, HALF, pair_features),
-        preferred_element_type=jnp.float32,
-    ).astype(jnp.bfloat16).reshape(rows, HALF, 2 * cols, HALF)
-    left_t = left.transpose(1, 3, 0, 2).reshape(rows, HALF, share)
-    right_part = jnp.einsum("icje,ics->jes", outer, left_t, preferred_element_type=jnp.float32)
-    right_part = (right_part / depth).astype(jnp.bfloat16)
-    right_part = right_part.reshape(2, cols * HALF, share)
-    right_part = jnp.concatenate([right_part[0], right_part[1]], axis=1)
-    moved = jnp.concatenate([gathered[:, rows:].reshape(chips * rows, 128), right_part], axis=0)
+    ).reshape(chips * 2 * own_rows, wide)
+
+    own = pair.transpose(1, 0, 2)
+    other = lax.ppermute(own, both, [(n, n ^ 1) for n in range(ni * nj)])
+    maps = couple_map.reshape(8, 4, 8, 4, pair_features)
+    map_right = maps.reshape(8, 4, HALF, pair_features).transpose(0, 2, 1, 3).reshape(256, 512)
+    outer_right = call(
+        outer_right_kernel, (wide, wide), [SMEM, VMEM, VMEM, VMEM], 2 * 256 * 512 * 4096
+    )(core.reshape(1), map_right, own, other)
+    moved = call(
+        functools.partial(right_kernel, 1.0 / depth), (wide, 128), [VMEM, VMEM], 1 << 28
+    )(outer_right, gathered)
+
     swap = [
         (p * nj + 2 * m + c, m * nj + 2 * p + c)
         for p in range(ni)
         for m in range(chips)
         for c in range(2)
     ]
+    (own, other, acts, incoming), moved = lax.optimization_barrier(
+        ((own, other, acts, incoming), moved)
+    )
     moved = lax.ppermute(moved, both, swap)
 
-    (acts, incoming), _ = lax.optimization_barrier(((acts, incoming), right_part))
     attn_in = lax.all_to_all(
         jnp.concatenate([acts, incoming], axis=1), "rj", 0, 0, tiled=True
     )
     acts_res = attn_in[:, :own_rows].reshape(depth, features)
     inc_res = attn_in[:, own_rows:].reshape(depth, features)
 
-    right = moved[: chips * rows].reshape(chips, 2 * cols, own_rows, HALF)
-    right_t = right.transpose(1, 3, 0, 2).reshape(2 * cols, HALF, share)
-    left_part = jnp.einsum("icje,jes->ics", outer, right_t, preferred_element_type=jnp.float32)
-    left_part = (left_part / depth).astype(jnp.bfloat16)
-    right_back = moved[chips * rows :]
-    right_back = jnp.concatenate([right_back[:, :share], right_back[:, share:]], axis=0)
-    sums = jnp.concatenate([left_part, right_back.reshape(rows, HALF, share)], axis=2)
-    sums = lax.all_to_all(sums, "rj", 0, 0, tiled=True)
+    is_even = core == 0
+    chip_pair = jnp.concatenate(
+        [jnp.where(is_even, own, other), jnp.where(is_even, other, own)], axis=0
+    ).transpose(1, 0, 2)
+    map_left = (
+        maps.reshape(HALF, 8, 4, pair_features).transpose(1, 0, 2, 3).reshape(256, 512)
+    )
+    outer_left = call(outer_left_kernel, (wide, wide), [VMEM, VMEM], 2 * 256 * 512 * 4096)(
+        map_left, chip_pair
+    )
+    sums = call(functools.partial(left_kernel, 1.0 / depth), (wide, 128), [VMEM, VMEM], 1 << 28)(
+        outer_left, moved
+    )
+    sums = lax.all_to_all(sums.reshape(rows, HALF, 128), "rj", 0, 0, tiled=True)
     sums = jnp.sum(
         sums.reshape(chips, 2, HALF, 2, share).astype(jnp.float32), axis=0
     ).astype(jnp.bfloat16)

time: 122 us -> 100 us (0.82)
  the two profiles are of different devices: /device:TPU:1 before, /device:TPU:129 now
where the time goes in v3:
time: 100 us; the launch traced here: 99.5 us
  starting transfers between devices  46.1 us (46%)
  waiting for transfers between devices  25 us (25%)
  blocking collectives  11.4 us (11%)
  local copies, waits for them, and re-layouts  6.82 us (7%)
  Pallas kernels  5.03 us (5%)
  matrix products  2.45 us (2%)
  other arithmetic  2.37 us (2%)
    all_to_all x1, starting transfers between devices, local(): sums = lax.all_to_all(sums.reshape(rows, HALF, 128), 'rj', 0, 0, tiled=True)  27.1 us
    ppermute x1, waiting for transfers between devices, local(): moved = lax.ppermute(moved, both, swap)  12.4 us
    all_to_all x1, blocking collectives, local(): lax.all_to_all(result.reshape(nj, own_rows, features), 'rj', 0, 0, tiled=...  11.4 us
    all_to_all x1, waiting for transfers between devices, local(): sums = lax.all_to_all(sums.reshape(rows, HALF, 128), 'rj', 0, 0, tiled=True)  10.2 us
    all_to_all x1, starting transfers between devices, local(): lax.all_to_all(jnp.broadcast_to(halves[None], (chips,) + halves.shape), '...  8.36 us
    all_to_all x1, starting transfers between devices, local(): lax.all_to_all(jnp.concatenate([acts, incoming], axis=1), 'rj', 0, 0, til...  5.95 us
    ppermute x1, starting transfers between devices, local(): other = lax.ppermute(own, both, [(n, n ^ 1) for n in range(ni * nj)])  2.87 us
    all_to_all x1, waiting for transfers between devices, local(): lax.all_to_all(jnp.broadcast_to(halves[None], (chips,) + halves.shape), '...  2.39 us
  transfers between devices with their start and end apart: 5, of which 3 were waited for; matrix products, arithmetic and copies ran while one was open for 4% of the time, Pallas kernels for 4%

profile of v3, /device:TPU:129, one launch (start us, length us, event | category | flops | bytes accessed | tf_op | source)
XLA Modules:
  0.0 99.5 jit_solution(14419138214622885589)
XLA Ops:
  0.0 0.0 copy-start
  0.0 0.9 copy.56
  0.9 0.8 copy.57
  1.7 0.1 broadcast_in_dim.4
  1.8 0.7 broadcast_in_dim.10
  2.6 8.4 %all-to-all-start = ((bf16[16,8,1024]{2,1,0:T(8,128)(2,1)}), bf16[16,8,1024]{2,1,0:T(8,128)(2,1)S(1)}, u32[]{:S(2)}, u32[]{:S(2)}) async-start(bf16[16,8,1024]{2,1,0:T(8,128)(2,1)} %broadcast_in_dim.10), calls=%async_computation | async-start | bytes 524288 | tf_op jit(solution)/shard_map/all_to_all | solution.py:177
  10.9 2.9 %collective-permute-start = (bf16[16,32,128]{2,0,1:T(8,128)(2,1)}, bf16[16,32,128]{2,0,1:T(8,128)(2,1)S(1)}, u32[]{:S(2)}, u32[]{:S(2)}) collective-permute-start(bf16[16,32,128]{2,0,1:T(8,128)(2,1)} %bitcast.115), channel_id=1, source_target_pairs={{0,1},{1,0},{2,3},{3,2},{4,5},{5,4},{6,7},{7,6},{8,9},{9,8},{10,11... | collective-permute-start | bytes 393224 | tf_op jit(solution)/shard_map/ppermute | solution.py:187
  13.8 0.9 copy.38.own_ref
  14.8 1.1 %copy.37 = bf16[8,4,32,128]{3,1,2,0:T(4,128)(2,1)S(1)} copy(bf16[8,4,32,128]{3,2,1,0:T(8,128)(2,1)} %bitcast.105) | data formatting | bytes 524288 | tf_op jit(solution)/shard_map/reshape;reshape | solution.py:189
  15.9 0.0 collective-permute-done
  15.9 0.0 copy-start.3
  16.0 0.6 copy-done.3
  16.6 1.5 %shard_map.91.outer_ref = bf16[1024,1024]{1,0:T(8,128)(2,1)S(1)} custom-call(s32[1]{0:T(128)} %bitcast.1.core_ref, bf16[256,512]{1,0:T(8,128)(2,1)S(1)} %bitcast.100, bf16[16,32,128]{2,1,0:T(8,128)(2,1)S(1)} %copy.38.own_ref, bf16[16,32,128]{2,1,0:T(8,128)(2,1)S(1)} %copy.39.other_ref), custom_call_target="tpu_custom_call" | custom-call | flops 1073741824 | bytes 4194304 | tf_op jit(solution)/shard_map/pallas_call | solution.py:190
  18.0 0.0 copy-start.1
  18.0 2.4 %all-to-all-done = bf16[16,8,1024]{2,1,0:T(8,128)(2,1)S(1)} async-done(((bf16[16,8,1024]{2,1,0:T(8,128)(2,1)}), bf16[16,8,1024]{2,1,0:T(8,128)(2,1)S(1)}, u32[]{:S(2)}, u32[]{:S(2)}) %all-to-all-start) | async-done | bytes 262176 | tf_op jit(solution)/shard_map/all_to_all | solution.py:177
  20.4 0.0 copy-start.5
  20.4 0.0 copy-start.6
  20.4 0.0 copy-start.2
  20.4 0.8 shard_map.92
  21.3 0.0 copy-done.5
  21.3 0.0 copy-done.6
  21.3 0.7 pad_maximum_fusion.1
  22.0 6.0 %all-to-all-start.1 = ((bf16[32,8,256]{2,1,0:T(8,128)(2,1)}), bf16[32,8,256]{2,1,0:T(8,128)(2,1)S(1)}, u32[]{:S(2)}, u32[]{:S(2)}) async-start(bf16[32,8,256]{2,1,0:T(8,128)(2,1)} %pad_maximum_fusion.1), calls=%async_computation.1 | async-start | bytes 262144 | tf_op jit(solution)/shard_map/all_to_all | solution.py:208
  28.0 0.0 copy-done.1
  28.0 0.1 copy.42
  28.1 1.9 %collective-permute-start.1 = (bf16[1024,128]{1,0:T(8,128)(2,1)S(1)}, bf16[1024,128]{1,0:T(8,128)(2,1)S(1)}, u32[]{:S(2)}, u32[]{:S(2)}) collective-permute-start(bf16[1024,128]{1,0:T(8,128)(2,1)S(1)} %shard_map.92), channel_id=1, source_target_pairs={{0,0},{1,1},{2,32},{3,33},{4,64},{5,65},{6,96},{7,97},{8,128},{9,1... | collective-permute-start | bytes 786440 | tf_op jit(solution)/shard_map/ppermute | solution.py:206
  30.1 0.0 copy-done.2
  30.1 0.9 broadcast_select_fusion.1
  31.0 1.3 %shard_map.93.outer_ref = bf16[1024,1024]{1,0:T(8,128)(2,1)S(1)} custom-call(bf16[256,512]{1,0:T(8,128)(2,1)S(1)} %bitcast.99, bf16[32,32,128]{2,1,0:T(8,128)(2,1)S(1)} %maximum_bitcast_fusion.pair_ref), custom_call_target="tpu_custom_call" | custom-call | flops 1073741824 | bytes 4194304 | tf_op jit(solution)/shard_map/pallas_call | solution.py:221
  32.4 12.4 %collective-permute-done.1.moved_ref = bf16[1024,128]{1,0:T(8,128)(2,1)S(1)} collective-permute-done((bf16[1024,128]{1,0:T(8,128)(2,1)S(1)}, bf16[1024,128]{1,0:T(8,128)(2,1)S(1)}, u32[]{:S(2)}, u32[]{:S(2)}) %collective-permute-start.1) | collective-permute-done | bytes 262176 | tf_op jit(solution)/shard_map/ppermute | solution.py:206
  44.8 1.4 %shard_map.94 = bf16[1024,128]{1,0:T(8,128)(2,1)} custom-call(bf16[1024,1024]{1,0:T(8,128)(2,1)S(1)} %shard_map.93.outer_ref, bf16[1024,128]{1,0:T(8,128)(2,1)S(1)} %collective-permute-done.1.moved_ref), custom_call_target="tpu_custom_call" | custom-call | flops 268435456 | bytes 4194304 | tf_op jit(solution)/shard_map/pallas_call | solution.py:224
  46.2 0.0 all-to-all-done.1
  46.2 27.1 %all-to-all-start.2 = ((bf16[32,32,128]{2,1,0:T(8,128)(2,1)}), bf16[32,32,128]{2,1,0:T(8,128)(2,1)S(1)}, u32[]{:S(2)}, u32[]{:S(2)}) async-start(bf16[32,32,128]{2,1,0:T(8,128)(2,1)} %bitcast.11), calls=%async_computation.2 | async-start | bytes 524288 | tf_op jit(solution)/shard_map/all_to_all | solution.py:227
  73.4 0.0 copy-done
  73.4 0.2 convolution_convert_fusion
  73.7 0.2 copy.45
  73.8 0.0 copy-start.7
  73.8 0.0 copy-start.4
  73.9 0.3 fusion.21
  74.2 10.2 %all-to-all-done.2 = bf16[32,32,128]{2,1,0:T(8,128)(2,1)S(1)} async-done(((bf16[32,32,128]{2,1,0:T(8,128)(2,1)}), bf16[32,32,128]{2,1,0:T(8,128)(2,1)S(1)}, u32[]{:S(2)}, u32[]{:S(2)}) %all-to-all-start.2) | async-done | bytes 262176 | tf_op jit(solution)/shard_map/all_to_all | solution.py:227
  84.4 0.2 reshape.59
  84.6 0.6 reduce_sum.30
  85.2 0.1 copy.43
  85.3 0.1 copy.44
  85.4 0.1 reshape.61
  85.5 0.0 copy-done.7
  85.5 0.1 fusion.11
  85.7 0.0 copy-done.4
  85.7 0.2 fusion.37
  85.9 0.3 fusion.27
  86.2 0.2 fusion.12
  86.4 0.3 fusion.13
  86.7 0.3 fusion.14
  86.9 0.2 fusion.15
  87.2 0.3 fusion.10
  87.5 11.4 %all_to_all.20 = bf16[32,4,256]{2,1,0:T(4,128)(2,1)S(1)} all-to-all(bf16[32,4,256]{2,1,0:T(4,128)(2,1)S(1)} %reshape.65), channel_id=1, replica_groups=mesh['ri'=16,'rj'=32] {'rj'}, dimensions={0} | all-to-all | bytes 131072 | tf_op jit(solution)/shard_map/all_to_all | solution.py:241
  98.9 0.6 copy.65
  (10 shorter events, 0.3 us)
Async XLA Ops:
  0.0 73.4 %copy-start = (bf16[256,1024]{1,0:T(8,128)(2,1)S(1)}, bf16[256,1024]{1,0:T(8,128)(2,1)}, u32[]{:S(2)}) copy-start(bf16[256,1024]{1,0:T(8,128)(2,1)} %param.16) | copy-start | bytes 1572868
  2.6 17.9 %all-to-all-start = ((bf16[16,8,1024]{2,1,0:T(8,128)(2,1)}), bf16[16,8,1024]{2,1,0:T(8,128)(2,1)S(1)}, u32[]{:S(2)}, u32[]{:S(2)}) async-start(bf16[16,8,1024]{2,1,0:T(8,128)(2,1)} %broadcast_in_dim.10), calls=%async_computation | async-start | bytes 524288 | tf_op jit(solution)/shard_map/all_to_all | solution.py:177
  10.9 5.0 %collective-permute-start = (bf16[16,32,128]{2,0,1:T(8,128)(2,1)}, bf16[16,32,128]{2,0,1:T(8,128)(2,1)S(1)}, u32[]{:S(2)}, u32[]{:S(2)}) collective-permute-start(bf16[16,32,128]{2,0,1:T(8,128)(2,1)} %bitcast.115), channel_id=1, source_target_pairs={{0,1},{1,0},{2,3},{3,2},{4,5},{5,4},{6,7},{7,6},{8,9},{9,8},{10,11... | collective-permute-start | bytes 393224 | tf_op jit(solution)/shard_map/ppermute | solution.py:187
  15.9 0.7 copy-start.3
  18.0 10.0 %copy-start.1 = (bf16[1024,128]{1,0:T(8,128)(2,1)S(1)}, bf16[1024,128]{1,0:T(8,128)(2,1)}, u32[]{:S(2)}) copy-start(bf16[1024,128]{1,0:T(8,128)(2,1)} %param.14) | copy-start | bytes 786436
  20.4 0.9 copy-start.5
  20.4 0.9 copy-start.6
  20.4 9.6 %copy-start.2 = (bf16[32,16,128]{2,1,0:T(8,128)(2,1)S(1)}, bf16[32,16,128]{2,1,0:T(8,128)(2,1)}, u32[]{:S(2)}) copy-start(bf16[32,16,128]{2,1,0:T(8,128)(2,1)} %param.9) | copy-start | bytes 393220
  22.0 24.2 %all-to-all-start.1 = ((bf16[32,8,256]{2,1,0:T(8,128)(2,1)}), bf16[32,8,256]{2,1,0:T(8,128)(2,1)S(1)}, u32[]{:S(2)}, u32[]{:S(2)}) async-start(bf16[32,8,256]{2,1,0:T(8,128)(2,1)} %pad_maximum_fusion.1), calls=%async_computation.1 | async-start | bytes 262144 | tf_op jit(solution)/shard_map/all_to_all | solution.py:208
  28.1 16.7 %collective-permute-start.1 = (bf16[1024,128]{1,0:T(8,128)(2,1)S(1)}, bf16[1024,128]{1,0:T(8,128)(2,1)S(1)}, u32[]{:S(2)}, u32[]{:S(2)}) collective-permute-start(bf16[1024,128]{1,0:T(8,128)(2,1)S(1)} %shard_map.92), channel_id=1, source_target_pairs={{0,0},{1,1},{2,32},{3,33},{4,64},{5,65},{6,96},{7,97},{8,128},{9,1... | collective-permute-start | bytes 786440 | tf_op jit(solution)/shard_map/ppermute | solution.py:206
  46.2 38.2 %all-to-all-start.2 = ((bf16[32,32,128]{2,1,0:T(8,128)(2,1)}), bf16[32,32,128]{2,1,0:T(8,128)(2,1)S(1)}, u32[]{:S(2)}, u32[]{:S(2)}) async-start(bf16[32,32,128]{2,1,0:T(8,128)(2,1)} %bitcast.11), calls=%async_computation.2 | async-start | bytes 524288 | tf_op jit(solution)/shard_map/all_to_all | solution.py:227
  73.8 11.7 %copy-start.7 = (bf16[256,64]{0,1:T(8,128)(2,1)S(1)}, bf16[256,64]{0,1:T(8,128)(2,1)}, u32[]{:S(2)}) copy-start(bf16[256,64]{0,1:T(8,128)(2,1)} %param.15) | copy-start | bytes 98308
  73.8 11.8 %copy-start.4 = (bf16[256,256]{1,0:T(8,128)(2,1)S(1)}, bf16[256,256]{1,0:T(8,128)(2,1)}, u32[]{:S(2)}) copy-start(bf16[256,256]{1,0:T(8,128)(2,1)} %param.17) | copy-start | bytes 393220

commit v4 on v3

--- a/solution.py
+++ b/solution.py
@@ -76,7 +76,41 @@
                 )
 
 
-def outer_right_kernel(core_ref, lhs_ref, own_ref, other_ref, out_ref):
+def factors_kernel(first_ref, second_ref, out_ref):
+    shape = (256, 1024)
+    copies = jnp.where(
+        lax.broadcasted_iota(jnp.int32, (HALF, 1024), 0)
+        == (lax.broadcasted_iota(jnp.int32, (HALF, 1024), 1) & 31),
+        1.0,
+        0.0,
+    ).astype(jnp.bfloat16)
+    both = jnp.concatenate([first_ref[...], second_ref[...]], axis=1)
+    tiled = lax.dot_general(
+        both, copies, (((0,), (0,)), ((), ())), preferred_element_type=jnp.float32
+    )
+    own_channel = (lax.broadcasted_iota(jnp.int32, shape, 0) & 31) == (
+        lax.broadcasted_iota(jnp.int32, shape, 1) >> 5
+    )
+    kept = jnp.where(own_channel, tiled, 0.0).astype(jnp.bfloat16)
+    rows = jnp.where(
+        (lax.broadcasted_iota(jnp.int32, (128, 256), 0) & 7)
+        == (lax.broadcasted_iota(jnp.int32, (128, 256), 1) >> 5),
+        1.0,
+        0.0,
+    ).astype(jnp.bfloat16)
+    out_ref[...] = jnp.dot(rows, kept, preferred_element_type=jnp.float32).astype(jnp.bfloat16)
+
+
+def outer_right_kernel(core_ref, map_ref, own_ref, other_ref, out_ref):
+    lhs = jnp.concatenate(
+        [
+            jnp.concatenate(
+                [map_ref[(h * 4 + g) * HALF : (h * 4 + g + 1) * HALF] for g in range(4)], axis=1
+            )
+            for h in range(8)
+        ],
+        axis=0,
+    )
     cols = own_ref.shape[0]
     core = core_ref[0]
     starts = [core * (cols * HALF), (1 - core) * (cols * HALF)]
@@ -85,7 +119,7 @@
         row = pl.multiple_of(starts[m] + n * HALF, HALF)
         out_ref[pl.ds(row, HALF), g * 128 : (g + 1) * 128] = block
 
-    outer_blocks(lhs_ref[...], [own_ref, other_ref], store)
+    outer_blocks(lhs, [own_ref, other_ref], store)
 
 
 def outer_left_kernel(lhs_ref, pair_ref, out_ref):
@@ -123,7 +157,7 @@
         ]
 
 
-def left_kernel(scale, outer_ref, moved_ref, out_ref):
+def left_kernel(scale, outer_ref, moved_ref, attn_ref, out_ref):
     right = jnp.concatenate(
         [moved_ref[512 + block * 64 : 576 + block * 64] for block in range(8)], axis=1
     )
@@ -133,8 +167,14 @@
     ) * scale
     packed = moved_ref[:512].astype(jnp.float32)
     is_left = lax.broadcasted_iota(jnp.int32, (512, 128), 1) < 64
-    out_ref[:512] = jnp.where(is_left, sums[:512], pltpu.roll(packed, 64, 1)).astype(jnp.bfloat16)
-    out_ref[512:] = jnp.where(is_left, sums[512:], packed).astype(jnp.bfloat16)
+    low = jnp.where(is_left, sums[:512], pltpu.roll(packed, 64, 1)).astype(jnp.bfloat16)
+    high = jnp.where(is_left, sums[512:], packed).astype(jnp.bfloat16)
+    half = out_ref.shape[0] // 2
+    for n in range(half):
+        out_ref[n, :HALF] = low[n * HALF : (n + 1) * HALF]
+        out_ref[n + half, :HALF] = high[n * HALF : (n + 1) * HALF]
+    for n in range(2 * half):
+        out_ref[n, HALF:] = attn_ref[n]
 
 
 def call(kernel, shape, specs, flops):
@@ -170,12 +210,14 @@
     features = incoming.shape[2]
     both = ("ri", "rj")
     wide = rows * HALF
-
-    halves = jnp.stack([first, second]).reshape(2, rows, own_rows, HALF)
-    halves = halves.transpose(0, 2, 3, 1).reshape(2 * own_rows, wide)
+    scale = 1.0 / depth
+
+    halves = call(factors_kernel, (chips * 2 * own_rows, wide), [VMEM, VMEM], 1 << 27)(
+        first, second
+    )
     groups = [[2 * m + c for m in range(chips)] for c in range(2)]
     gathered = lax.all_to_all(
-        jnp.broadcast_to(halves[None], (chips,) + halves.shape),
+        halves.reshape(chips, 2 * own_rows, wide),
         "rj",
         0,
         0,
@@ -186,12 +228,11 @@
     own = pair.transpose(1, 0, 2)
     other = lax.ppermute(own, both, [(n, n ^ 1) for n in range(ni * nj)])
     maps = couple_map.reshape(8, 4, 8, 4, pair_features)
-    map_right = maps.reshape(8, 4, HALF, pair_features).transpose(0, 2, 1, 3).reshape(256, 512)
     outer_right = call(
         outer_right_kernel, (wide, wide), [SMEM, VMEM, VMEM, VMEM], 2 * 256 * 512 * 4096
-    )(core.reshape(1), map_right, own, other)
+    )(core.reshape(1), couple_map, own, other)
     moved = call(
-        functools.partial(right_kernel, 1.0 / depth), (wide, 128), [VMEM, VMEM], 1 << 28
+        functools.partial(right_kernel, scale), (wide, 128), [VMEM, VMEM], 1 << 28
     )(outer_right, gathered)
 
     swap = [
@@ -200,16 +241,8 @@
         for m in range(chips)
         for c in range(2)
     ]
-    (own, other, acts, incoming), moved = lax.optimization_barrier(
-        ((own, other, acts, incoming), moved)
-    )
+    (own, other), moved = lax.optimization_barrier(((own, other), moved))
     moved = lax.ppermute(moved, both, swap)
-
-    attn_in = lax.all_to_all(
-        jnp.concatenate([acts, incoming], axis=1), "rj", 0, 0, tiled=True
-    )
-    acts_res = attn_in[:, :own_rows].reshape(depth, features)
-    inc_res = attn_in[:, own_rows:].reshape(depth, features)
 
     is_even = core == 0
     chip_pair = jnp.concatenate(
@@ -221,10 +254,16 @@
     outer_left = call(outer_left_kernel, (wide, wide), [VMEM, VMEM], 2 * 256 * 512 * 4096)(
         map_left, chip_pair
     )
-    sums = call(functools.partial(left_kernel, 1.0 / depth), (wide, 128), [VMEM, VMEM], 1 << 28)(
-        outer_left, moved
-    )
-    sums = lax.all_to_all(sums.reshape(rows, HALF, 128), "rj", 0, 0, tiled=True)
+    attn_in = jnp.concatenate(
+        [acts.reshape(rows, 2 * own_rows, 128), incoming.reshape(rows, 2 * own_rows, 128)], axis=1
+    )
+    sums = call(
+        functools.partial(left_kernel, scale), (rows, HALF + 16, 128), [VMEM, VMEM, VMEM], 1 << 28
+    )(outer_left, moved, attn_in)
+    received = lax.all_to_all(sums, "rj", 0, 0, tiled=True)
+    sums = received[:, :HALF]
+    acts_res = received[:, HALF : HALF + 8].reshape(depth, features)
+    inc_res = received[:, HALF + 8 :].reshape(depth, features)
     sums = jnp.sum(
         sums.reshape(chips, 2, HALF, 2, share).astype(jnp.float32), axis=0
     ).astype(jnp.bfloat16)

time: 100 us -> 95.4 us (0.954)
  blocking collectives: 11.4 us -> 52.9 us
  starting transfers between devices: 46.1 us -> 13.1 us
  waiting for transfers between devices: 25 us -> 12.6 us
  other arithmetic: 2.37 us -> 0.75 us
    all_to_all x0 -> x1, blocking collectives: none -> 41.4 us  [local(): received = lax.all_to_all(sums, 'rj', 0, 0, tiled=True)]
    all_to_all x3 -> x1, starting transfers between devices: 41.4 us -> 8.35 us  [local(): lax.all_to_all(halves.reshape(chips, 2 * own_rows, wide), 'rj', 0, 0, axi...]
    all_to_all x3 -> x1, waiting for transfers between devices: 12.6 us -> 0.74 us  [local(): lax.all_to_all(halves.reshape(chips, 2 * own_rows, wide), 'rj', 0, 0, axi...]
    another operation x3 -> x0, local copies, waits for them, and re-layouts: 2.77 us -> none  [the longest x2 1.68 us: local(): halves = jnp.stack([first, second]).reshape(2, rows, own_rows, HALF)]
    unnamed x19 -> x26, local copies, waits for them, and re-layouts: 1.35 us -> 3.67 us
    pallas_call x2 -> x3, Pallas kernels: 2.24 us -> 2.73 us  [the longest x1 1.2 us: local(): call(factors_kernel, (chips * 2 * own_rows, wide), [VMEM, VMEM], 1 << 27)]
  transfers between devices with their start and end apart: 5 -> 3, of which waited for: 3 -> 2; matrix products, arithmetic and copies ran while one was open for 4% -> 3% of each run, Pallas kernels for 4% -> 3%
where the time goes in v4:
time: 95.4 us; the launch traced here: 95 us
  blocking collectives  52.9 us (55%)
  starting transfers between devices  13.1 us (14%)
  waiting for transfers between devices  12.6 us (13%)
  local copies, waits for them, and re-layouts  7.2 us (8%)
  Pallas kernels  5.52 us (6%)
  matrix products  2.46 us (3%)
    all_to_all x1, blocking collectives, local(): received = lax.all_to_all(sums, 'rj', 0, 0, tiled=True)  41.4 us
    ppermute x1, waiting for transfers between devices, local(): moved = lax.ppermute(moved, both, swap)  11.9 us
    all_to_all x1, blocking collectives, local(): lax.all_to_all(result.reshape(nj, own_rows, features), 'rj', 0, 0, tiled=...  11.5 us
    all_to_all x1, starting transfers between devices, local(): lax.all_to_all(halves.reshape(chips, 2 * own_rows, wide), 'rj', 0, 0, axi...  8.35 us
    unnamed x26, local copies, waits for them, and re-layouts  3.67 us
    ppermute x1, starting transfers between devices, local(): other = lax.ppermute(own, both, [(n, n ^ 1) for n in range(ni * nj)])  2.87 us
    ppermute x1, starting transfers between devices, local(): moved = lax.ppermute(moved, both, swap)  1.92 us
  transfers between devices with their start and end apart: 3, of which 2 were waited for; matrix products, arithmetic and copies ran while one was open for 3% of the time, Pallas kernels for 3%

profile of v4, /device:TPU:129, one launch (start us, length us, event | category | flops | bytes accessed | tf_op | source)
XLA Modules:
  0.0 95.0 jit_solution(9594252068080856526)
XLA Ops:
  0.0 0.0 copy-start
  0.0 0.0 copy-start.1
  0.0 0.0 copy-start.3
  0.0 0.8 copy-done.3
  0.8 0.0 copy-start.4
  0.8 0.7 copy-done.4
  1.5 0.0 copy-start.9
  1.5 0.0 copy-start.10
  1.5 1.2 %shard_map.92 = bf16[128,1024]{1,0:T(8,128)(2,1)} custom-call(bf16[32,128]{1,0:T(8,128)(2,1)S(1)} %copy-done.3, bf16[32,128]{1,0:T(8,128)(2,1)S(1)} %copy-done.4), custom_call_target="tpu_custom_call" | custom-call | flops 134217728 | bytes 4194304 | tf_op jit(solution)/shard_map/pallas_call | solution.py:215
  2.7 8.4 %all-to-all-start = ((bf16[16,8,1024]{2,1,0:T(8,128)(2,1)}), bf16[16,8,1024]{2,1,0:T(8,128)(2,1)S(1)}, u32[]{:S(2)}, u32[]{:S(2)}) async-start(bf16[16,8,1024]{2,1,0:T(8,128)(2,1)} %bitcast.4), calls=%async_computation | async-start | bytes 524288 | tf_op jit(solution)/shard_map/all_to_all | solution.py:219
  11.0 2.9 %collective-permute-start = (bf16[16,32,128]{2,0,1:T(8,128)(2,1)}, bf16[16,32,128]{2,0,1:T(8,128)(2,1)S(1)}, u32[]{:S(2)}, u32[]{:S(2)}) collective-permute-start(bf16[16,32,128]{2,0,1:T(8,128)(2,1)} %bitcast.99), channel_id=1, source_target_pairs={{0,1},{1,0},{2,3},{3,2},{4,5},{5,4},{6,7},{7,6},{8,9},{9,8},{10,11... | collective-permute-start | bytes 393224 | tf_op jit(solution)/shard_map/ppermute | solution.py:229
  13.9 1.6 %copy.34.own_ref = bf16[16,32,128]{2,1,0:T(8,128)(2,1)} copy(bf16[16,32,128]{2,0,1:T(8,128)(2,1)} %bitcast.100) | data formatting | bytes 262144 | tf_op jit(solution)/shard_map/transpose | solution.py:228
  15.5 1.0 %copy.33 = bf16[32,8,4,128]{3,2,0,1:T(4,128)(2,1)S(1)} copy(bf16[32,8,4,128]{3,2,1,0:T(4,128)(2,1)} %bitcast.86) | data formatting | bytes 524288 | tf_op jit(solution)/shard_map/reshape;reshape | solution.py:252
  16.6 0.0 copy-done.9
  16.7 0.0 copy-done.10
  16.7 0.0 collective-permute-done
  16.7 0.0 copy-start.6
  16.8 0.6 copy-done.6
  17.4 0.0 copy-done.1
  17.4 0.0 copy-start.2
  17.4 0.9 copy-done.2
  18.3 1.5 %shard_map.91.outer_ref = bf16[1024,1024]{1,0:T(8,128)(2,1)S(1)} custom-call(s32[1]{0:T(128)} %bitcast.3.core_ref, bf16[1024,128]{1,0:T(8,128)(2,1)S(1)} %copy-done.1, bf16[16,32,128]{2,1,0:T(8,128)(2,1)S(1)} %copy-done.2, bf16[16,32,128]{2,1,0:T(8,128)(2,1)S(1)} %copy.35.other_ref), custom_call_target="tpu_custom_call" | custom-call | flops 1073741824 | bytes 4194304 | tf_op jit(solution)/shard_map/pallas_call | solution.py:231
  19.8 0.0 copy-start.5
  19.8 0.0 copy-start.7
  19.8 0.7 all-to-all-done
  20.5 0.8 shard_map.93
  21.4 1.9 %collective-permute-start.1 = (bf16[1024,128]{1,0:T(8,128)(2,1)S(1)}, bf16[1024,128]{1,0:T(8,128)(2,1)S(1)}, u32[]{:S(2)}, u32[]{:S(2)}) collective-permute-start(bf16[1024,128]{1,0:T(8,128)(2,1)S(1)} %shard_map.93), channel_id=1, source_target_pairs={{0,0},{1,1},{2,32},{3,33},{4,64},{5,65},{6,96},{7,97},{8,128},{9,1... | collective-permute-start | bytes 786440 | tf_op jit(solution)/shard_map/ppermute | solution.py:245
  23.3 0.0 copy-done.5
  23.3 0.0 copy-done.7
  23.4 1.3 %shard_map.94.outer_ref = bf16[1024,1024]{1,0:T(8,128)(2,1)S(1)} custom-call(bf16[256,512]{1,0:T(8,128)(2,1)S(1)} %bitcast.87, bf16[32,32,128]{2,1,0:T(8,128)(2,1)S(1)} %maximum_bitcast_fusion.pair_ref), custom_call_target="tpu_custom_call" | custom-call | flops 1073741824 | bytes 4194304 | tf_op jit(solution)/shard_map/pallas_call | solution.py:254
  24.7 11.9 %collective-permute-done.1.moved_ref = bf16[1024,128]{1,0:T(8,128)(2,1)S(1)} collective-permute-done((bf16[1024,128]{1,0:T(8,128)(2,1)S(1)}, bf16[1024,128]{1,0:T(8,128)(2,1)S(1)}, u32[]{:S(2)}, u32[]{:S(2)}) %collective-permute-start.1) | collective-permute-done | bytes 262176 | tf_op jit(solution)/shard_map/ppermute | solution.py:245
  36.6 0.7 shard_map.95
  37.3 41.4 %all_to_all.15 = bf16[32,48,128]{2,1,0:T(8,128)(2,1)S(1)} all-to-all(bf16[32,48,128]{2,1,0:T(8,128)(2,1)S(1)} %shard_map.95), channel_id=1, replica_groups=mesh['ri'=16,'rj'=32] {'rj'}, dimensions={0} | all-to-all | bytes 786432 | tf_op jit(solution)/shard_map/all_to_all | solution.py:263
  78.7 0.2 reshape.57
  79.0 0.6 reduce_sum.30
  79.6 0.1 copy.36
  79.7 0.1 copy.37
  79.8 0.1 reshape.59
  79.9 0.0 copy-start.11
  80.0 0.0 copy-done
  80.0 0.0 copy-start.8
  80.0 0.2 convolution_convert_fusion
  80.3 0.2 copy.38
  80.4 0.3 fusion.20
  80.8 0.0 copy-done.11
  80.8 0.1 fusion.36
  81.0 0.0 copy-done.8
  81.0 0.2 fusion.37
  81.1 0.3 fusion.26
  81.4 0.2 fusion.11
  81.7 0.3 fusion.12
  82.0 0.3 fusion.13
  82.2 0.2 fusion.14
  82.5 0.3 fusion.10
  82.8 11.5 %all_to_all.16 = bf16[32,4,256]{2,1,0:T(4,128)(2,1)S(1)} all-to-all(bf16[32,4,256]{2,1,0:T(4,128)(2,1)S(1)} %reshape.63), channel_id=1, replica_groups=mesh['ri'=16,'rj'=32] {'rj'}, dimensions={0} | all-to-all | bytes 131072 | tf_op jit(solution)/shard_map/all_to_all | solution.py:280
  94.3 0.6 copy.53
  (14 shorter events, 0.4 us)
Async XLA Ops:
  0.0 80.0 %copy-start = (bf16[256,1024]{1,0:T(8,128)(2,1)S(1)}, bf16[256,1024]{1,0:T(8,128)(2,1)}, u32[]{:S(2)}) copy-start(bf16[256,1024]{1,0:T(8,128)(2,1)} %param.16) | copy-start | bytes 1572868
  0.0 17.4 %copy-start.1 = (bf16[1024,128]{1,0:T(8,128)(2,1)S(1)}, bf16[1024,128]{1,0:T(8,128)(2,1)}, u32[]{:S(2)}) copy-start(bf16[1024,128]{1,0:T(8,128)(2,1)} %map_ref.1) | copy-start | bytes 786436
  0.0 0.8 copy-start.3
  0.8 0.7 copy-start.4
  1.5 15.1 %copy-start.9 = (bf16[32,4,256]{2,1,0:T(4,128)(2,1)S(1)}, bf16[32,4,256]{2,1,0:T(4,128)(2,1)}, u32[]{:S(2)}) copy-start(bf16[32,4,256]{2,1,0:T(4,128)(2,1)} %param.13) | copy-start | bytes 196612
  1.5 15.2 %copy-start.10 = (bf16[32,4,256]{2,1,0:T(4,128)(2,1)S(1)}, bf16[32,4,256]{2,1,0:T(4,128)(2,1)}, u32[]{:S(2)}) copy-start(bf16[32,4,256]{2,1,0:T(4,128)(2,1)} %param.12) | copy-start | bytes 196612
  2.7 17.8 %all-to-all-start = ((bf16[16,8,1024]{2,1,0:T(8,128)(2,1)}), bf16[16,8,1024]{2,1,0:T(8,128)(2,1)S(1)}, u32[]{:S(2)}, u32[]{:S(2)}) async-start(bf16[16,8,1024]{2,1,0:T(8,128)(2,1)} %bitcast.4), calls=%async_computation | async-start | bytes 524288 | tf_op jit(solution)/shard_map/all_to_all | solution.py:219
  11.0 5.7 %collective-permute-start = (bf16[16,32,128]{2,0,1:T(8,128)(2,1)}, bf16[16,32,128]{2,0,1:T(8,128)(2,1)S(1)}, u32[]{:S(2)}, u32[]{:S(2)}) collective-permute-start(bf16[16,32,128]{2,0,1:T(8,128)(2,1)} %bitcast.99), channel_id=1, source_target_pairs={{0,1},{1,0},{2,3},{3,2},{4,5},{5,4},{6,7},{7,6},{8,9},{9,8},{10,11... | collective-permute-start | bytes 393224 | tf_op jit(solution)/shard_map/ppermute | solution.py:229
  16.7 0.7 copy-start.6
  17.4 0.9 copy-start.2
  19.8 3.5 %copy-start.5 = (bf16[32,16,128]{2,1,0:T(8,128)(2,1)S(1)}, bf16[32,16,128]{2,1,0:T(8,128)(2,1)}, u32[]{:S(2)}) copy-start(bf16[32,16,128]{2,1,0:T(8,128)(2,1)} %param.9) | copy-start | bytes 393220
  19.8 3.5 %copy-start.7 = (bf16[16,32,128]{2,0,1:T(8,128)(2,1)S(1)}, bf16[16,32,128]{2,0,1:T(8,128)(2,1)}, u32[]{:S(2)}) copy-start(bf16[16,32,128]{2,0,1:T(8,128)(2,1)} %copy-done.6) | copy-start | bytes 393220
  21.4 15.2 %collective-permute-start.1 = (bf16[1024,128]{1,0:T(8,128)(2,1)S(1)}, bf16[1024,128]{1,0:T(8,128)(2,1)S(1)}, u32[]{:S(2)}, u32[]{:S(2)}) collective-permute-start(bf16[1024,128]{1,0:T(8,128)(2,1)S(1)} %shard_map.93), channel_id=1, source_target_pairs={{0,0},{1,1},{2,32},{3,33},{4,64},{5,65},{6,96},{7,97},{8,128},{9,1... | collective-permute-start | bytes 786440 | tf_op jit(solution)/shard_map/ppermute | solution.py:245
  79.9 0.9 copy-start.11
  80.0 0.9 copy-start.8

commit v5 on v4

--- a/solution.py
+++ b/solution.py
@@ -13,6 +13,42 @@
 VMEM = pl.BlockSpec(memory_space=pltpu.VMEM)
 SMEM = pl.BlockSpec(memory_space=pltpu.SMEM)
 LIMIT = 40 * 1024 * 1024
+SOURCE = (
+    (0, 3, 5, 4, 11, 10, 9, 14, 13, 15, 12, 8, 6, 7, 1, 2),
+    (3, 2, 0, 1, 9, 15, 11, 10, 13, 8, 12, 14, 6, 7, 4, 5),
+    (6, 7, 1, 2, 13, 11, 8, 9, 10, 15, 12, 14, 0, 3, 4, 5),
+    (2, 3, 4, 1, 10, 11, 8, 9, 13, 14, 15, 12, 5, 7, 0, 6),
+    (7, 6, 1, 2, 5, 11, 8, 4, 14, 15, 9, 10, 3, 0, 12, 13),
+    (3, 8, 7, 0, 10, 5, 4, 6, 15, 12, 11, 9, 1, 2, 14, 13),
+    (5, 3, 0, 4, 6, 7, 8, 10, 9, 11, 12, 13, 14, 15, 1, 2),
+    (2, 4, 5, 1, 7, 8, 9, 6, 10, 11, 12, 13, 14, 15, 3, 0),
+    (15, 12, 0, 1, 3, 2, 4, 5, 9, 10, 11, 8, 6, 7, 13, 14),
+    (13, 14, 2, 1, 3, 4, 0, 6, 10, 11, 5, 9, 7, 12, 15, 8),
+    (2, 3, 13, 14, 1, 6, 7, 0, 11, 4, 5, 10, 15, 8, 9, 12),
+    (2, 3, 15, 12, 6, 7, 0, 1, 10, 11, 4, 5, 13, 14, 8, 9),
+    (10, 12, 15, 13, 3, 2, 0, 1, 6, 7, 4, 5, 14, 11, 8, 9),
+    (11, 15, 8, 10, 5, 3, 0, 1, 2, 6, 7, 4, 14, 13, 12, 9),
+    (9, 11, 8, 12, 6, 7, 4, 5, 2, 0, 3, 1, 10, 15, 13, 14),
+    (9, 14, 12, 13, 2, 3, 1, 0, 5, 4, 7, 6, 11, 10, 8, 15),
+)
+TARGET = (
+    (0, 3, 5, 4, 11, 10, 9, 14, 13, 15, 12, 8, 6, 7, 1, 2),
+    (3, 2, 0, 1, 9, 15, 11, 10, 13, 8, 12, 14, 6, 7, 4, 5),
+    (6, 7, 1, 2, 13, 11, 8, 9, 10, 15, 12, 14, 0, 3, 4, 5),
+    (2, 3, 4, 1, 10, 11, 8, 9, 13, 14, 15, 12, 5, 7, 0, 6),
+    (7, 6, 1, 2, 5, 11, 8, 4, 14, 15, 9, 10, 3, 0, 12, 13),
+    (3, 8, 7, 0, 10, 5, 4, 6, 15, 12, 11, 9, 1, 2, 14, 13),
+    (5, 3, 0, 4, 6, 7, 8, 10, 9, 11, 12, 13, 14, 15, 1, 2),
+    (2, 4, 5, 1, 7, 8, 9, 6, 10, 11, 12, 13, 14, 15, 3, 0),
+    (15, 12, 0, 1, 3, 2, 4, 5, 9, 10, 11, 8, 6, 7, 13, 14),
+    (13, 14, 2, 1, 3, 4, 0, 6, 10, 11, 5, 9, 7, 12, 15, 8),
+    (2, 3, 13, 14, 1, 6, 7, 0, 11, 4, 5, 10, 15, 8, 9, 12),
+    (2, 3, 15, 12, 6, 7, 0, 1, 10, 11, 4, 5, 13, 14, 8, 9),
+    (10, 12, 15, 13, 3, 2, 0, 1, 6, 7, 4, 5, 14, 11, 8, 9),
+    (11, 15, 8, 10, 5, 3, 0, 1, 2, 6, 7, 4, 14, 13, 12, 9),
+    (9, 11, 8, 12, 6, 7, 4, 5, 2, 0, 3, 1, 10, 15, 13, 14),
+    (9, 14, 12, 13, 2, 3, 1, 0, 5, 4, 7, 6, 11, 10, 8, 15),
+)
 
 
 def attention_backward(acts, grad, qkvg_map, result_map):
@@ -55,13 +91,12 @@
     return (grad.astype(jnp.float32) + back).astype(jnp.bfloat16)
 
 
-def outer_blocks(lhs, pieces, store):
-    count = pieces[0].shape[0]
+def outer_blocks(lhs, count, pieces, store):
     zero = jnp.zeros((HALF, 128), jnp.bfloat16)
     for n in range(count):
         stacked = []
         for piece in pieces:
-            x = piece[n]
+            x = piece(n)
             for g in range(4):
                 stacked.append(
                     jnp.concatenate([x if h == g else zero for h in range(4)], axis=1)
@@ -111,7 +146,7 @@
         ],
         axis=0,
     )
-    cols = own_ref.shape[0]
+    cols = own_ref.shape[1]
     core = core_ref[0]
     starts = [core * (cols * HALF), (1 - core) * (cols * HALF)]
 
@@ -119,20 +154,29 @@
         row = pl.multiple_of(starts[m] + n * HALF, HALF)
         out_ref[pl.ds(row, HALF), g * 128 : (g + 1) * 128] = block
 
-    outer_blocks(lhs, [own_ref, other_ref], store)
-
-
-def outer_left_kernel(lhs_ref, pair_ref, out_ref):
-    half = pair_ref.shape[0] // 2
+    outer_blocks(
+        lhs, cols, [lambda n: own_ref[:, n, :], lambda n: other_ref[:, n, :]], store
+    )
+
+
+def outer_left_kernel(core_ref, lhs_ref, own_ref, other_ref, out_ref):
+    half = own_ref.shape[0] // 2
+    is_even = core_ref[0] == 0
+
+    def columns(i):
+        own, other = own_ref[i], other_ref[i]
+        return jnp.concatenate(
+            [jnp.where(is_even, own, other), jnp.where(is_even, other, own)], axis=0
+        )
 
     def store(m, n, g, block):
         row = (m * half + n) * HALF
         out_ref[row : row + HALF, g * 128 : (g + 1) * 128] = block
 
-    outer_blocks(lhs_ref[...], [pair_ref.at[:half], pair_ref.at[half:]], store)
-
-
-def right_kernel(scale, outer_ref, gathered_ref, out_ref):
+    outer_blocks(lhs_ref[...], half, [columns, lambda n: columns(half + n)], store)
+
+
+def right_kernel(scale, outer_ref, gathered_ref, out_ref, factors_ref):
     to = lax.broadcasted_iota(jnp.int32, (128, 128), 0)
     at = lax.broadcasted_iota(jnp.int32, (128, 128), 1)
     want = ((to & 63) >> 2) * 8 + (to >> 6) * 4 + (to & 3)
@@ -150,22 +194,22 @@
         outer_ref[512:], jnp.concatenate([none, left], axis=0), NT,
         preferred_element_type=jnp.float32,
     )
-    out_ref[:512] = ((low + high) * scale).astype(jnp.bfloat16)
+    out_ref[...] = ((low + high) * scale).astype(jnp.bfloat16)
     for block in range(8):
-        out_ref[512 + block * 64 : 576 + block * 64] = sorted_rows[
+        factors_ref[block * 64 : 64 + block * 64] = sorted_rows[
             64:, block * 128 : (block + 1) * 128
         ]
 
 
-def left_kernel(scale, outer_ref, moved_ref, attn_ref, out_ref):
+def left_kernel(scale, outer_ref, factors_ref, right_ref, attn_ref, out_ref):
     right = jnp.concatenate(
-        [moved_ref[512 + block * 64 : 576 + block * 64] for block in range(8)], axis=1
+        [factors_ref[block * 64 : 64 + block * 64] for block in range(8)], axis=1
     )
     sums = lax.dot_general(
         outer_ref[...], jnp.concatenate([right, jnp.zeros_like(right)], axis=0), NT,
         preferred_element_type=jnp.float32,
     ) * scale
-    packed = moved_ref[:512].astype(jnp.float32)
+    packed = right_ref[...].astype(jnp.float32)
     is_left = lax.broadcasted_iota(jnp.int32, (512, 128), 1) < 64
     low = jnp.where(is_left, sums[:512], pltpu.roll(packed, 64, 1)).astype(jnp.bfloat16)
     high = jnp.where(is_left, sums[512:], packed).astype(jnp.bfloat16)
@@ -177,12 +221,14 @@
         out_ref[n, HALF:] = attn_ref[n]
 
 
-def call(kernel, shape, specs, flops):
+def call(kernel, shapes, specs, flops):
+    many = isinstance(shapes, list)
+    out = [jax.ShapeDtypeStruct(x, jnp.bfloat16) for x in (shapes if many else [shapes])]
     return pl.pallas_call(
         kernel,
-        out_shape=jax.ShapeDtypeStruct(shape, jnp.bfloat16),
+        out_shape=out if many else out[0],
         in_specs=specs,
-        out_specs=VMEM,
+        out_specs=[VMEM] * len(out) if many else VMEM,
         compiler_params=pltpu.CompilerParams(vmem_limit_bytes=LIMIT),
         cost_estimate=pl.CostEstimate(flops=flops, bytes_accessed=4 << 20, transcendentals=0),
     )
@@ -225,41 +271,41 @@
         tiled=True,
     ).reshape(chips * 2 * own_rows, wide)
 
-    own = pair.transpose(1, 0, 2)
-    other = lax.ppermute(own, both, [(n, n ^ 1) for n in range(ni * nj)])
-    maps = couple_map.reshape(8, 4, 8, 4, pair_features)
+    other = lax.ppermute(pair, both, [(n, n ^ 1) for n in range(ni * nj)])
     outer_right = call(
         outer_right_kernel, (wide, wide), [SMEM, VMEM, VMEM, VMEM], 2 * 256 * 512 * 4096
-    )(core.reshape(1), couple_map, own, other)
-    moved = call(
-        functools.partial(right_kernel, scale), (wide, 128), [VMEM, VMEM], 1 << 28
+    )(core.reshape(1), couple_map, pair, other)
+    right_part, factors = call(
+        functools.partial(right_kernel, scale), [(wide // 2, 128)] * 2, [VMEM, VMEM], 1 << 28
     )(outer_right, gathered)
 
-    swap = [
-        (p * nj + 2 * m + c, m * nj + 2 * p + c)
-        for p in range(ni)
-        for m in range(chips)
-        for c in range(2)
-    ]
-    (own, other), moved = lax.optimization_barrier(((own, other), moved))
-    moved = lax.ppermute(moved, both, swap)
-
-    is_even = core == 0
-    chip_pair = jnp.concatenate(
-        [jnp.where(is_even, own, other), jnp.where(is_even, other, own)], axis=0
-    ).transpose(1, 0, 2)
+    (pair, other, couple_map), right_part = lax.optimization_barrier(
+        ((pair, other, couple_map), right_part)
+    )
+    places = [(p, m, c) for p in range(ni) for m in range(chips) for c in range(2)]
+    factors = lax.ppermute(
+        factors,
+        both,
+        [(m * nj + 2 * SOURCE[m][p] + c, p * nj + 2 * m + c) for p, m, c in places],
+    )
+    right_part = lax.ppermute(
+        right_part,
+        both,
+        [(p * nj + 2 * m + c, m * nj + 2 * TARGET[m][p] + c) for p, m, c in places],
+    )
+
     map_left = (
-        maps.reshape(HALF, 8, 4, pair_features).transpose(1, 0, 2, 3).reshape(256, 512)
-    )
-    outer_left = call(outer_left_kernel, (wide, wide), [VMEM, VMEM], 2 * 256 * 512 * 4096)(
-        map_left, chip_pair
-    )
+        couple_map.reshape(HALF, 8, 4, pair_features).transpose(1, 0, 2, 3).reshape(256, 512)
+    )
+    outer_left = call(
+        outer_left_kernel, (wide, wide), [SMEM, VMEM, VMEM, VMEM], 2 * 256 * 512 * 4096
+    )(core.reshape(1), map_left, pair, other)
     attn_in = jnp.concatenate(
         [acts.reshape(rows, 2 * own_rows, 128), incoming.reshape(rows, 2 * own_rows, 128)], axis=1
     )
     sums = call(
-        functools.partial(left_kernel, scale), (rows, HALF + 16, 128), [VMEM, VMEM, VMEM], 1 << 28
-    )(outer_left, moved, attn_in)
+        functools.partial(left_kernel, scale), (rows, HALF + 16, 128), [VMEM] * 4, 1 << 28
+    )(outer_left, factors, right_part, attn_in)
     received = lax.all_to_all(sums, "rj", 0, 0, tiled=True)
     sums = received[:, :HALF]
     acts_res = received[:, HALF : HALF + 8].reshape(depth, features)

time: 95.4 us -> 92.8 us (0.973)
  the two profiles are of different devices: /device:TPU:129 before, /device:TPU:1 now
where the time goes in v5:
time: 92.8 us; the launch traced here: 92.3 us
  blocking collectives  62 us (67%)
  starting transfers between devices  13.7 us (15%)
  local copies, waits for them, and re-layouts  6.63 us (7%)
  Pallas kernels  5.49 us (6%)
  matrix products  2.45 us (3%)
  waiting for transfers between devices  1.01 us (1%)
    all_to_all x1, blocking collectives, local(): received = lax.all_to_all(sums, 'rj', 0, 0, tiled=True)  50.5 us
    all_to_all x1, blocking collectives, local(): lax.all_to_all(result.reshape(nj, own_rows, features), 'rj', 0, 0, tiled=...  11.5 us
    all_to_all x1, starting transfers between devices, local(): lax.all_to_all(halves.reshape(chips, 2 * own_rows, wide), 'rj', 0, 0, axi...  9.2 us
    unnamed x20, local copies, waits for them, and re-layouts  4 us
    ppermute x1, starting transfers between devices, local(): other = lax.ppermute(pair, both, [(n, n ^ 1) for n in range(ni * nj)])  3.13 us
  transfers between devices with their start and end apart: 4, of which 1 were waited for; matrix products, arithmetic and copies ran while one was open for 2% of the time, Pallas kernels for 3%

profile of v5, /device:TPU:1, one launch (start us, length us, event | category | flops | bytes accessed | tf_op | source)
XLA Modules:
  0.0 92.3 jit_solution(13524524117966033720)
XLA Ops:
  0.0 0.0 copy-start
  0.0 0.0 copy-start.5
  0.0 0.8 copy-done.5
  0.8 0.0 copy-start.6
  0.8 0.7 copy-done.6
  1.5 1.2 %shard_map.92 = bf16[128,1024]{1,0:T(8,128)(2,1)} custom-call(bf16[32,128]{1,0:T(8,128)(2,1)S(1)} %copy-done.5, bf16[32,128]{1,0:T(8,128)(2,1)S(1)} %copy-done.6), custom_call_target="tpu_custom_call" | custom-call | flops 134217728 | bytes 4194304 | tf_op jit(solution)/shard_map/pallas_call | solution.py:261
  2.6 9.2 %all-to-all-start = ((bf16[16,8,1024]{2,1,0:T(8,128)(2,1)}), bf16[16,8,1024]{2,1,0:T(8,128)(2,1)S(1)}, u32[]{:S(2)}, u32[]{:S(2)}) async-start(bf16[16,8,1024]{2,1,0:T(8,128)(2,1)} %bitcast.1), calls=%async_computation | async-start | bytes 524288 | tf_op jit(solution)/shard_map/all_to_all | solution.py:265
  11.8 3.1 %collective-permute-start = (bf16[32,16,128]{2,1,0:T(8,128)(2,1)}, bf16[32,16,128]{2,1,0:T(8,128)(2,1)S(1)}, u32[]{:S(2)}, u32[]{:S(2)}) collective-permute-start(bf16[32,16,128]{2,1,0:T(8,128)(2,1)} %own_ref.2), channel_id=1, source_target_pairs={{0,1},{1,0},{2,3},{3,2},{4,5},{5,4},{6,7},{7,6},{8,9},{9,8},{10,11... | collective-permute-start | bytes 393224 | tf_op jit(solution)/shard_map/ppermute | solution.py:274
  15.0 0.9 reshape.60
  15.9 0.9 reshape.61
  16.7 0.0 collective-permute-done.other_ref
  16.7 0.0 copy-start.1
  16.8 0.9 %copy-done.1 = bf16[1024,128]{1,0:T(8,128)(2,1)S(1)} copy-done((bf16[1024,128]{1,0:T(8,128)(2,1)S(1)}, bf16[1024,128]{1,0:T(8,128)(2,1)}, u32[]{:S(2)}) %copy-start.1) | copy-done | bytes 262168
  17.7 0.0 copy-start.3
  17.7 0.9 copy-done.3
  18.6 1.4 %shard_map.91.outer_ref = bf16[1024,1024]{1,0:T(8,128)(2,1)S(1)} custom-call(s32[1]{0:T(128)} %bitcast.core_ref, bf16[1024,128]{1,0:T(8,128)(2,1)S(1)} %copy-done.1, bf16[32,16,128]{2,1,0:T(8,128)(2,1)S(1)} %copy-done.3, bf16[32,16,128]{2,1,0:T(8,128)(2,1)S(1)} %collective-permute-done.other_ref), custom_call_target="tpu_custom_call" | custom-call | flops 1073741824 | bytes 4194304 | tf_op jit(solution)/shard_map/pallas_call | solution.py:275
  20.1 0.0 copy-start.2
  20.1 0.0 copy-start.4
  20.1 1.0 %all-to-all-done = bf16[16,8,1024]{2,1,0:T(8,128)(2,1)S(1)} async-done(((bf16[16,8,1024]{2,1,0:T(8,128)(2,1)}), bf16[16,8,1024]{2,1,0:T(8,128)(2,1)S(1)}, u32[]{:S(2)}, u32[]{:S(2)}) %all-to-all-start) | async-done | bytes 262176 | tf_op jit(solution)/shard_map/all_to_all | solution.py:265
  21.1 0.8 shard_map.93
  21.9 0.7 collective-permute-start.2
  22.6 0.7 collective-permute-start.1
  23.3 0.0 copy-done.2
  23.3 0.1 copy.29
  23.5 0.0 copy-done.4
  23.5 1.3 %shard_map.94.outer_ref = bf16[1024,1024]{1,0:T(8,128)(2,1)S(1)} custom-call(s32[1]{0:T(128)} %bitcast.core_ref, bf16[256,512]{1,0:T(8,128)(2,1)S(1)} %bitcast.84, bf16[32,16,128]{2,1,0:T(8,128)(2,1)S(1)} %copy-done.4, bf16[32,16,128]{2,1,0:T(8,128)(2,1)S(1)} %collective-permute-done.other_ref), custom_call_target="tpu_custom_call" | custom-call | flops 1073741824 | bytes 4194304 | tf_op jit(solution)/shard_map/pallas_call | solution.py:300
  24.8 0.0 collective-permute-done.2.right_ref
  24.8 0.0 collective-permute-done.1.factors_ref
  24.9 0.7 shard_map.95
  25.5 50.5 %all_to_all.15 = bf16[32,48,128]{2,1,0:T(8,128)(2,1)S(1)} all-to-all(bf16[32,48,128]{2,1,0:T(8,128)(2,1)S(1)} %shard_map.95), channel_id=1, replica_groups=mesh['ri'=16,'rj'=32] {'rj'}, dimensions={0} | all-to-all | bytes 786432 | tf_op jit(solution)/shard_map/all_to_all | solution.py:309
  76.1 0.2 reshape.62
  76.3 0.6 reduce_sum.30
  76.9 0.1 copy.30
  77.0 0.1 copy.31
  77.1 0.1 reshape.64
  77.3 0.0 copy-start.8
  77.3 0.0 copy-done
  77.4 0.0 copy-start.7
  77.4 0.2 convolution_convert_fusion
  77.6 0.2 copy.32
  77.8 0.3 fusion.20
  78.1 0.0 copy-done.8
  78.1 0.1 fusion.36
  78.3 0.0 copy-done.7
  78.3 0.2 fusion.37
  78.5 0.3 fusion.26
  78.8 0.2 fusion.11
  79.0 0.3 fusion.12
  79.3 0.3 fusion.13
  79.6 0.2 fusion.14
  79.8 0.3 fusion.10
  80.2 11.5 %all_to_all.16 = bf16[32,4,256]{2,1,0:T(4,128)(2,1)S(1)} all-to-all(bf16[32,4,256]{2,1,0:T(4,128)(2,1)S(1)} %reshape.68), channel_id=1, replica_groups=mesh['ri'=16,'rj'=32] {'rj'}, dimensions={0} | all-to-all | bytes 131072 | tf_op jit(solution)/shard_map/all_to_all | solution.py:326
  91.7 0.6 copy.47
  (9 shorter events, 0.2 us)
Async XLA Ops:
  0.0 77.3 %copy-start = (bf16[256,1024]{1,0:T(8,128)(2,1)S(1)}, bf16[256,1024]{1,0:T(8,128)(2,1)}, u32[]{:S(2)}) copy-start(bf16[256,1024]{1,0:T(8,128)(2,1)} %param.16) | copy-start | bytes 1572868
  0.0 0.8 copy-start.5
  0.8 0.7 copy-start.6
  2.6 18.4 %all-to-all-start = ((bf16[16,8,1024]{2,1,0:T(8,128)(2,1)}), bf16[16,8,1024]{2,1,0:T(8,128)(2,1)S(1)}, u32[]{:S(2)}, u32[]{:S(2)}) async-start(bf16[16,8,1024]{2,1,0:T(8,128)(2,1)} %bitcast.1), calls=%async_computation | async-start | bytes 524288 | tf_op jit(solution)/shard_map/all_to_all | solution.py:265
  11.8 4.9 %collective-permute-start = (bf16[32,16,128]{2,1,0:T(8,128)(2,1)}, bf16[32,16,128]{2,1,0:T(8,128)(2,1)S(1)}, u32[]{:S(2)}, u32[]{:S(2)}) collective-permute-start(bf16[32,16,128]{2,1,0:T(8,128)(2,1)} %own_ref.2), channel_id=1, source_target_pairs={{0,1},{1,0},{2,3},{3,2},{4,5},{5,4},{6,7},{7,6},{8,9},{9,8},{10,11... | collective-permute-start | bytes 393224 | tf_op jit(solution)/shard_map/ppermute | solution.py:274
  16.7 1.0 %copy-start.1 = (bf16[1024,128]{1,0:T(8,128)(2,1)S(1)}, bf16[1024,128]{1,0:T(8,128)(2,1)}, u32[]{:S(2)}) copy-start(bf16[1024,128]{1,0:T(8,128)(2,1)} %map_ref.1) | copy-start | bytes 786436
  17.7 0.9 copy-start.3
  20.1 3.3 %copy-start.2 = (bf16[1024,128]{1,0:T(8,128)(2,1)S(1)}, bf16[1024,128]{1,0:T(8,128)(2,1)}, u32[]{:S(2)}) copy-start(bf16[1024,128]{1,0:T(8,128)(2,1)} %map_ref.1) | copy-start | bytes 786436
  20.1 3.4 %copy-start.4 = (bf16[32,16,128]{2,1,0:T(8,128)(2,1)S(1)}, bf16[32,16,128]{2,1,0:T(8,128)(2,1)}, u32[]{:S(2)}) copy-start(bf16[32,16,128]{2,1,0:T(8,128)(2,1)} %own_ref.2) | copy-start | bytes 393220
  21.9 2.9 %collective-permute-start.2 = (bf16[512,128]{1,0:T(8,128)(2,1)S(1)}, bf16[512,128]{1,0:T(8,128)(2,1)S(1)}, u32[]{:S(2)}, u32[]{:S(2)}) collective-permute-start(bf16[512,128]{1,0:T(8,128)(2,1)S(1)} %get-tuple-element.16), channel_id=1, source_target_pairs={{0,0},{1,1},{2,38},{3,39},{4,76},{5,77},{6,100},{7,101},{8,142},{9... | collective-permute-start | bytes 393224 | tf_op jit(solution)/shard_map/ppermute | solution.py:291
  22.6 2.2 %collective-permute-start.1 = (bf16[512,128]{1,0:T(8,128)(2,1)S(1)}, bf16[512,128]{1,0:T(8,128)(2,1)S(1)}, u32[]{:S(2)}, u32[]{:S(2)}) collective-permute-start(bf16[512,128]{1,0:T(8,128)(2,1)S(1)} %get-tuple-element.15), channel_id=1, source_target_pairs={{0,0},{1,1},{38,2},{39,3},{76,4},{77,5},{100,6},{101,7},{142,8},{1... | collective-permute-start | bytes 393224 | tf_op jit(solution)/shard_map/ppermute | solution.py:286
  77.3 0.9 copy-start.8
  77.4 0.9 %copy-start.7 = (bf16[256,256]{1,0:T(8,128)(2,1)S(1)}, bf16[256,256]{1,0:T(8,128)(2,1)}, u32[]{:S(2)}) copy-start(bf16[256,256]{1,0:T(8,128)(2,1)} %param.17) | copy-start | bytes 393220

commit v6 on v5

--- a/solution.py
+++ b/solution.py
@@ -147,6 +147,17 @@
         axis=0,
     )
     cols = own_ref.shape[1]
+    count = own_ref.shape[0] * cols
+    to = lax.broadcasted_iota(jnp.int32, (count, count), 0)
+    at = lax.broadcasted_iota(jnp.int32, (count, count), 1)
+    order = jnp.where(at == (to & 31) * cols + (to >> 5), 1.0, 0.0).astype(jnp.bfloat16)
+    turned = jnp.dot(
+        order,
+        jnp.concatenate(
+            [own_ref[...].reshape(count, 128), other_ref[...].reshape(count, 128)], axis=1
+        ),
+        preferred_element_type=jnp.float32,
+    ).astype(jnp.bfloat16)
     core = core_ref[0]
     starts = [core * (cols * HALF), (1 - core) * (cols * HALF)]
 
@@ -155,7 +166,8 @@
         out_ref[pl.ds(row, HALF), g * 128 : (g + 1) * 128] = block
 
     outer_blocks(
-        lhs, cols, [lambda n: own_ref[:, n, :], lambda n: other_ref[:, n, :]], store
+        lhs, cols, [lambda n: turned[n * HALF : (n + 1) * HALF, :128],
+         lambda n: turned[n * HALF : (n + 1) * HALF, 128:]], store
     )
 
 

time: 92.8 us -> 92.8 us (level)
  no operation moved by 1% of the time
where the time goes in v6:
time: 92.8 us; the launch traced here: 92.3 us
  blocking collectives  62 us (67%)
  starting transfers between devices  13.7 us (15%)
  local copies, waits for them, and re-layouts  6.63 us (7%)
  Pallas kernels  5.94 us (6%)
  matrix products  2.46 us (3%)
    all_to_all x1, blocking collectives, local(): received = lax.all_to_all(sums, 'rj', 0, 0, tiled=True)  50.5 us
    all_to_all x1, blocking collectives, local(): lax.all_to_all(result.reshape(nj, own_rows, features), 'rj', 0, 0, tiled=...  11.5 us
    all_to_all x1, starting transfers between devices, local(): lax.all_to_all(halves.reshape(chips, 2 * own_rows, wide), 'rj', 0, 0, axi...  9.2 us
    unnamed x20, local copies, waits for them, and re-layouts  4 us
    ppermute x1, starting transfers between devices, local(): other = lax.ppermute(pair, both, [(n, n ^ 1) for n in range(ni * nj)])  3.13 us
    pallas_call x1, Pallas kernels, local(): call(outer_right_kernel, (wide, wide), [SMEM, VMEM, VMEM, VMEM], 2 * 256...  1.89 us
  transfers between devices with their start and end apart: 4, of which 1 were waited for; matrix products, arithmetic and copies ran while one was open for 2% of the time, Pallas kernels for 3%

profile of v6, /device:TPU:1, one launch (start us, length us, event | category | flops | bytes accessed | tf_op | source)
XLA Modules:
  0.0 92.3 jit_solution(17871696586304390901)
XLA Ops:
  0.0 0.0 copy-start
  0.0 0.0 copy-start.5
  0.0 0.8 copy-done.5
  0.8 0.0 copy-start.6
  0.8 0.7 copy-done.6
  1.5 1.2 %shard_map.92 = bf16[128,1024]{1,0:T(8,128)(2,1)} custom-call(bf16[32,128]{1,0:T(8,128)(2,1)S(1)} %copy-done.5, bf16[32,128]{1,0:T(8,128)(2,1)S(1)} %copy-done.6), custom_call_target="tpu_custom_call" | custom-call | flops 134217728 | bytes 4194304 | tf_op jit(solution)/shard_map/pallas_call | solution.py:273
  2.6 9.2 %all-to-all-start = ((bf16[16,8,1024]{2,1,0:T(8,128)(2,1)}), bf16[16,8,1024]{2,1,0:T(8,128)(2,1)S(1)}, u32[]{:S(2)}, u32[]{:S(2)}) async-start(bf16[16,8,1024]{2,1,0:T(8,128)(2,1)} %bitcast.1), calls=%async_computation | async-start | bytes 524288 | tf_op jit(solution)/shard_map/all_to_all | solution.py:277
  11.8 3.1 %collective-permute-start = (bf16[32,16,128]{2,1,0:T(8,128)(2,1)}, bf16[32,16,128]{2,1,0:T(8,128)(2,1)S(1)}, u32[]{:S(2)}, u32[]{:S(2)}) collective-permute-start(bf16[32,16,128]{2,1,0:T(8,128)(2,1)} %own_ref.2), channel_id=1, source_target_pairs={{0,1},{1,0},{2,3},{3,2},{4,5},{5,4},{6,7},{7,6},{8,9},{9,8},{10,11... | collective-permute-start | bytes 393224 | tf_op jit(solution)/shard_map/ppermute | solution.py:286
  15.0 0.9 reshape.60
  15.9 0.9 reshape.61
  16.7 0.0 collective-permute-done.other_ref
  16.7 0.0 copy-start.1
  16.8 0.9 %copy-done.1 = bf16[1024,128]{1,0:T(8,128)(2,1)S(1)} copy-done((bf16[1024,128]{1,0:T(8,128)(2,1)S(1)}, bf16[1024,128]{1,0:T(8,128)(2,1)}, u32[]{:S(2)}) %copy-start.1) | copy-done | bytes 262168
  17.7 0.0 copy-start.3
  17.7 0.9 copy-done.3
  18.6 1.9 %shard_map.91.outer_ref = bf16[1024,1024]{1,0:T(8,128)(2,1)S(1)} custom-call(s32[1]{0:T(128)} %bitcast.core_ref, bf16[1024,128]{1,0:T(8,128)(2,1)S(1)} %copy-done.1, bf16[32,16,128]{2,1,0:T(8,128)(2,1)S(1)} %copy-done.3, bf16[32,16,128]{2,1,0:T(8,128)(2,1)S(1)} %collective-permute-done.other_ref), custom_call_target="tpu_custom_call" | custom-call | flops 1073741824 | bytes 4194304 | tf_op jit(solution)/shard_map/pallas_call | solution.py:287
  20.5 0.0 copy-start.2
  20.5 0.0 copy-start.4
  20.5 0.6 all-to-all-done
  21.1 0.8 shard_map.93
  21.9 0.7 collective-permute-start.2
  22.6 0.7 collective-permute-start.1
  23.3 0.0 copy-done.2
  23.3 0.1 copy.29
  23.5 0.0 copy-done.4
  23.5 1.3 %shard_map.94.outer_ref = bf16[1024,1024]{1,0:T(8,128)(2,1)S(1)} custom-call(s32[1]{0:T(128)} %bitcast.core_ref, bf16[256,512]{1,0:T(8,128)(2,1)S(1)} %bitcast.84, bf16[32,16,128]{2,1,0:T(8,128)(2,1)S(1)} %copy-done.4, bf16[32,16,128]{2,1,0:T(8,128)(2,1)S(1)} %collective-permute-done.other_ref), custom_call_target="tpu_custom_call" | custom-call | flops 1073741824 | bytes 4194304 | tf_op jit(solution)/shard_map/pallas_call | solution.py:312
  24.8 0.0 collective-permute-done.2.right_ref
  24.8 0.0 collective-permute-done.1.factors_ref
  24.9 0.7 shard_map.95
  25.5 50.5 %all_to_all.15 = bf16[32,48,128]{2,1,0:T(8,128)(2,1)S(1)} all-to-all(bf16[32,48,128]{2,1,0:T(8,128)(2,1)S(1)} %shard_map.95), channel_id=1, replica_groups=mesh['ri'=16,'rj'=32] {'rj'}, dimensions={0} | all-to-all | bytes 786432 | tf_op jit(solution)/shard_map/all_to_all | solution.py:321
  76.1 0.2 reshape.62
  76.3 0.6 reduce_sum.30
  77.0 0.1 copy.30
  77.1 0.1 copy.31
  77.1 0.1 reshape.64
  77.3 0.0 copy-start.8
  77.4 0.0 copy-done
  77.4 0.0 copy-start.7
  77.4 0.2 convolution_convert_fusion
  77.6 0.2 copy.32
  77.8 0.3 fusion.20
  78.1 0.0 copy-done.8
  78.2 0.1 fusion.36
  78.3 0.0 copy-done.7
  78.3 0.2 fusion.37
  78.5 0.3 fusion.26
  78.8 0.2 fusion.11
  79.0 0.3 fusion.12
  79.3 0.3 fusion.13
  79.6 0.2 fusion.14
  79.8 0.3 fusion.10
  80.2 11.5 %all_to_all.16 = bf16[32,4,256]{2,1,0:T(4,128)(2,1)S(1)} all-to-all(bf16[32,4,256]{2,1,0:T(4,128)(2,1)S(1)} %reshape.68), channel_id=1, replica_groups=mesh['ri'=16,'rj'=32] {'rj'}, dimensions={0} | all-to-all | bytes 131072 | tf_op jit(solution)/shard_map/all_to_all | solution.py:338
  91.7 0.6 copy.47
  (9 shorter events, 0.2 us)
Async XLA Ops:
  0.0 77.4 %copy-start = (bf16[256,1024]{1,0:T(8,128)(2,1)S(1)}, bf16[256,1024]{1,0:T(8,128)(2,1)}, u32[]{:S(2)}) copy-start(bf16[256,1024]{1,0:T(8,128)(2,1)} %param.16) | copy-start | bytes 1572868
  0.0 0.8 copy-start.5
  0.8 0.7 copy-start.6
  2.6 18.4 %all-to-all-start = ((bf16[16,8,1024]{2,1,0:T(8,128)(2,1)}), bf16[16,8,1024]{2,1,0:T(8,128)(2,1)S(1)}, u32[]{:S(2)}, u32[]{:S(2)}) async-start(bf16[16,8,1024]{2,1,0:T(8,128)(2,1)} %bitcast.1), calls=%async_computation | async-start | bytes 524288 | tf_op jit(solution)/shard_map/all_to_all | solution.py:277
  11.8 4.9 %collective-permute-start = (bf16[32,16,128]{2,1,0:T(8,128)(2,1)}, bf16[32,16,128]{2,1,0:T(8,128)(2,1)S(1)}, u32[]{:S(2)}, u32[]{:S(2)}) collective-permute-start(bf16[32,16,128]{2,1,0:T(8,128)(2,1)} %own_ref.2), channel_id=1, source_target_pairs={{0,1},{1,0},{2,3},{3,2},{4,5},{5,4},{6,7},{7,6},{8,9},{9,8},{10,11... | collective-permute-start | bytes 393224 | tf_op jit(solution)/shard_map/ppermute | solution.py:286
  16.7 1.0 %copy-start.1 = (bf16[1024,128]{1,0:T(8,128)(2,1)S(1)}, bf16[1024,128]{1,0:T(8,128)(2,1)}, u32[]{:S(2)}) copy-start(bf16[1024,128]{1,0:T(8,128)(2,1)} %map_ref.1) | copy-start | bytes 786436
  17.7 0.9 copy-start.3
  20.5 2.8 %copy-start.2 = (bf16[1024,128]{1,0:T(8,128)(2,1)S(1)}, bf16[1024,128]{1,0:T(8,128)(2,1)}, u32[]{:S(2)}) copy-start(bf16[1024,128]{1,0:T(8,128)(2,1)} %map_ref.1) | copy-start | bytes 786436
  20.5 3.0 %copy-start.4 = (bf16[32,16,128]{2,1,0:T(8,128)(2,1)S(1)}, bf16[32,16,128]{2,1,0:T(8,128)(2,1)}, u32[]{:S(2)}) copy-start(bf16[32,16,128]{2,1,0:T(8,128)(2,1)} %own_ref.2) | copy-start | bytes 393220
  21.9 2.9 %collective-permute-start.2 = (bf16[512,128]{1,0:T(8,128)(2,1)S(1)}, bf16[512,128]{1,0:T(8,128)(2,1)S(1)}, u32[]{:S(2)}, u32[]{:S(2)}) collective-permute-start(bf16[512,128]{1,0:T(8,128)(2,1)S(1)} %get-tuple-element.16), channel_id=1, source_target_pairs={{0,0},{1,1},{2,38},{3,39},{4,76},{5,77},{6,100},{7,101},{8,142},{9... | collective-permute-start | bytes 393224 | tf_op jit(solution)/shard_map/ppermute | solution.py:303
  22.6 2.2 %collective-permute-start.1 = (bf16[512,128]{1,0:T(8,128)(2,1)S(1)}, bf16[512,128]{1,0:T(8,128)(2,1)S(1)}, u32[]{:S(2)}, u32[]{:S(2)}) collective-permute-start(bf16[512,128]{1,0:T(8,128)(2,1)S(1)} %get-tuple-element.15), channel_id=1, source_target_pairs={{0,0},{1,1},{38,2},{39,3},{76,4},{77,5},{100,6},{101,7},{142,8},{1... | collective-permute-start | bytes 393224 | tf_op jit(solution)/shard_map/ppermute | solution.py:298
  77.3 0.9 copy-start.8
  77.4 0.9 %copy-start.7 = (bf16[256,256]{1,0:T(8,128)(2,1)S(1)}, bf16[256,256]{1,0:T(8,128)(2,1)}, u32[]{:S(2)}) copy-start(bf16[256,256]{1,0:T(8,128)(2,1)} %param.17) | copy-start | bytes 393220

commit v7 on v6

--- a/solution.py
+++ b/solution.py
@@ -213,7 +213,7 @@
         ]
 
 
-def left_kernel(scale, outer_ref, factors_ref, right_ref, attn_ref, out_ref):
+def left_kernel(scale, outer_ref, factors_ref, right_ref, out_ref):
     right = jnp.concatenate(
         [factors_ref[block * 64 : 64 + block * 64] for block in range(8)], axis=1
     )
@@ -229,8 +229,6 @@
     for n in range(half):
         out_ref[n, :HALF] = low[n * HALF : (n + 1) * HALF]
         out_ref[n + half, :HALF] = high[n * HALF : (n + 1) * HALF]
-    for n in range(2 * half):
-        out_ref[n, HALF:] = attn_ref[n]
 
 
 def call(kernel, shapes, specs, flops):
@@ -291,8 +289,8 @@
         functools.partial(right_kernel, scale), [(wide // 2, 128)] * 2, [VMEM, VMEM], 1 << 28
     )(outer_right, gathered)
 
-    (pair, other, couple_map), right_part = lax.optimization_barrier(
-        ((pair, other, couple_map), right_part)
+    (pair, other, couple_map, acts, incoming), right_part = lax.optimization_barrier(
+        ((pair, other, couple_map, acts, incoming), right_part)
     )
     places = [(p, m, c) for p in range(ni) for m in range(chips) for c in range(2)]
     factors = lax.ppermute(
@@ -310,18 +308,17 @@
         couple_map.reshape(HALF, 8, 4, pair_features).transpose(1, 0, 2, 3).reshape(256, 512)
     )
     outer_left = call(
-        outer_left_kernel, (wide, wide), [SMEM, VMEM, VMEM, VMEM], 2 * 256 * 512 * 4096
+        outer_left_kernel, (wide, wide), [SMEM, VMEM, VMEM, VMEM], 1 << 33
     )(core.reshape(1), map_left, pair, other)
-    attn_in = jnp.concatenate(
-        [acts.reshape(rows, 2 * own_rows, 128), incoming.reshape(rows, 2 * own_rows, 128)], axis=1
-    )
+    attn_in = lax.all_to_all(
+        jnp.concatenate([acts, incoming], axis=1), "rj", 0, 0, tiled=True
+    )
+    acts_res = attn_in[:, :own_rows].reshape(depth, features)
+    inc_res = attn_in[:, own_rows:].reshape(depth, features)
     sums = call(
-        functools.partial(left_kernel, scale), (rows, HALF + 16, 128), [VMEM] * 4, 1 << 28
-    )(outer_left, factors, right_part, attn_in)
-    received = lax.all_to_all(sums, "rj", 0, 0, tiled=True)
-    sums = received[:, :HALF]
-    acts_res = received[:, HALF : HALF + 8].reshape(depth, features)
-    inc_res = received[:, HALF + 8 :].reshape(depth, features)
+        functools.partial(left_kernel, scale), (rows, HALF, 128), [VMEM] * 3, 1 << 28
+    )(outer_left, factors, right_part)
+    sums = lax.all_to_all(sums, "rj", 0, 0, tiled=True)
     sums = jnp.sum(
         sums.reshape(chips, 2, HALF, 2, share).astype(jnp.float32), axis=0
     ).astype(jnp.bfloat16)

time: 92.8 us -> 91 us (0.981)
  blocking collectives: 62 us -> 11.4 us
  starting transfers between devices: 13.7 us -> 44.3 us
  waiting for transfers between devices: 0.56 us -> 18.3 us
  local copies, waits for them, and re-layouts: 6.63 us -> 4.88 us
  Pallas kernels: 5.94 us -> 7.32 us
    all_to_all x1 -> x0, blocking collectives: 50.5 us -> none  [local(): received = lax.all_to_all(sums, 'rj', 0, 0, tiled=True)]
    all_to_all x0 -> x2, starting transfers between devices: none -> 29.8 us  [the longest x1 20.3 us: local(): lax.all_to_all(jnp.concatenate([acts, incoming], axis=1), 'rj', 0, 0, til...]
    all_to_all x0 -> x2, waiting for transfers between devices: none -> 15.9 us  [the longest x1 10.2 us: local(): sums = lax.all_to_all(sums, 'rj', 0, 0, tiled=True)]
    reshape x3 -> x1, local copies, waits for them, and re-layouts: 1.77 us -> 0.02 us  [local(): acts_res = attn_in[:, :own_rows].reshape(depth, features)]
    ppermute x1, waiting for transfers between devices: 0.01 us -> 1.16 us  [local(): other = lax.ppermute(pair, both, [(n, n ^ 1) for n in range(ni * nj)])]
    unnamed x20 -> x24, local copies, waits for them, and re-layouts: 4 us -> 4.01 us
  transfers between devices with their start and end apart: 4 -> 6, of which waited for: 1 -> 4; matrix products, arithmetic and copies ran while one was open for 2% -> 2% of each run, Pallas kernels for 3% -> 5%
where the time goes in v7:
time: 91 us; the launch traced here: 90.3 us
  starting transfers between devices  44.3 us (49%)
  waiting for transfers between devices  18.3 us (20%)
  blocking collectives  11.4 us (13%)
  Pallas kernels  7.32 us (8%)
  local copies, waits for them, and re-layouts  4.88 us (5%)
  matrix products  2.46 us (3%)
  other arithmetic  1.41 us (2%)
    all_to_all x1, starting transfers between devices, local(): lax.all_to_all(jnp.concatenate([acts, incoming], axis=1), 'rj', 0, 0, til...  20.3 us
    all_to_all x1, blocking collectives, local(): lax.all_to_all(result.reshape(nj, own_rows, features), 'rj', 0, 0, tiled=...  11.4 us
    all_to_all x1, waiting for transfers between devices, local(): sums = lax.all_to_all(sums, 'rj', 0, 0, tiled=True)  10.2 us
    all_to_all x1, starting transfers between devices, local(): sums = lax.all_to_all(sums, 'rj', 0, 0, tiled=True)  9.46 us
    all_to_all x1, starting transfers between devices, local(): lax.all_to_all(halves.reshape(chips, 2 * own_rows, wide), 'rj', 0, 0, axi...  9.2 us
    all_to_all x1, waiting for transfers between devices, local(): lax.all_to_all(jnp.concatenate([acts, incoming], axis=1), 'rj', 0, 0, til...  5.75 us
    unnamed x24, local copies, waits for them, and re-layouts  4.01 us
    ppermute x1, starting transfers between devices, local(): other = lax.ppermute(pair, both, [(n, n ^ 1) for n in range(ni * nj)])  3.13 us
  transfers between devices with their start and end apart: 6, of which 4 were waited for; matrix products, arithmetic and copies ran while one was open for 2% of the time, Pallas kernels for 5%

profile of v7, /device:TPU:1, one launch (start us, length us, event | category | flops | bytes accessed | tf_op | source)
XLA Modules:
  0.0 90.3 jit_solution(6904915418878506970)
XLA Ops:
  0.0 0.0 copy-start
  0.0 0.0 copy-start.5
  0.0 0.8 copy-done.5
  0.8 0.0 copy-start.6
  0.8 0.7 copy-done.6
  1.5 1.2 %shard_map.92 = bf16[128,1024]{1,0:T(8,128)(2,1)} custom-call(bf16[32,128]{1,0:T(8,128)(2,1)S(1)} %copy-done.5, bf16[32,128]{1,0:T(8,128)(2,1)S(1)} %copy-done.6), custom_call_target="tpu_custom_call" | custom-call | flops 134217728 | bytes 4194304 | tf_op jit(solution)/shard_map/pallas_call | solution.py:271
  2.7 9.2 %all-to-all-start = ((bf16[16,8,1024]{2,1,0:T(8,128)(2,1)}), bf16[16,8,1024]{2,1,0:T(8,128)(2,1)S(1)}, u32[]{:S(2)}, u32[]{:S(2)}) async-start(bf16[16,8,1024]{2,1,0:T(8,128)(2,1)} %bitcast.1), calls=%async_computation | async-start | bytes 524288 | tf_op jit(solution)/shard_map/all_to_all | solution.py:275
  11.9 3.1 %collective-permute-start = (bf16[32,16,128]{2,1,0:T(8,128)(2,1)}, bf16[32,16,128]{2,1,0:T(8,128)(2,1)S(1)}, u32[]{:S(2)}, u32[]{:S(2)}) collective-permute-start(bf16[32,16,128]{2,1,0:T(8,128)(2,1)} %own_ref.2), channel_id=1, source_target_pairs={{0,1},{1,0},{2,3},{3,2},{4,5},{5,4},{6,7},{7,6},{8,9},{9,8},{10,11... | collective-permute-start | bytes 393224 | tf_op jit(solution)/shard_map/ppermute | solution.py:284
  15.0 1.2 %collective-permute-done.other_ref = bf16[32,16,128]{2,1,0:T(8,128)(2,1)S(1)} collective-permute-done((bf16[32,16,128]{2,1,0:T(8,128)(2,1)}, bf16[32,16,128]{2,1,0:T(8,128)(2,1)S(1)}, u32[]{:S(2)}, u32[]{:S(2)}) %collective-permute-start) | collective-permute-done | bytes 131104 | tf_op jit(solution)/shard_map/ppermute | solution.py:284
  16.2 0.0 copy-start.1
  16.2 0.9 %copy-done.1 = bf16[1024,128]{1,0:T(8,128)(2,1)S(1)} copy-done((bf16[1024,128]{1,0:T(8,128)(2,1)S(1)}, bf16[1024,128]{1,0:T(8,128)(2,1)}, u32[]{:S(2)}) %copy-start.1) | copy-done | bytes 262168
  17.1 0.0 copy-start.3
  17.1 0.9 copy-done.3
  18.0 1.9 %shard_map.91.outer_ref = bf16[1024,1024]{1,0:T(8,128)(2,1)S(1)} custom-call(s32[1]{0:T(128)} %bitcast.core_ref, bf16[1024,128]{1,0:T(8,128)(2,1)S(1)} %copy-done.1, bf16[32,16,128]{2,1,0:T(8,128)(2,1)S(1)} %copy-done.3, bf16[32,16,128]{2,1,0:T(8,128)(2,1)S(1)} %collective-permute-done.other_ref), custom_call_target="tpu_custom_call" | custom-call | flops 1073741824 | bytes 4194304 | tf_op jit(solution)/shard_map/pallas_call | solution.py:285
  19.9 0.0 copy-start.2
  19.9 0.0 copy-start.4
  19.9 1.2 %all-to-all-done = bf16[16,8,1024]{2,1,0:T(8,128)(2,1)S(1)} async-done(((bf16[16,8,1024]{2,1,0:T(8,128)(2,1)}), bf16[16,8,1024]{2,1,0:T(8,128)(2,1)S(1)}, u32[]{:S(2)}, u32[]{:S(2)}) %all-to-all-start) | async-done | bytes 262176 | tf_op jit(solution)/shard_map/all_to_all | solution.py:275
  21.1 0.0 copy-start.8
  21.1 0.0 copy-start.9
  21.1 1.5 %shard_map.93 = (bf16[512,128]{1,0:T(8,128)(2,1)}, bf16[512,128]{1,0:T(8,128)(2,1)S(1)}) custom-call(bf16[1024,1024]{1,0:T(8,128)(2,1)S(1)} %shard_map.91.outer_ref, bf16[128,1024]{1,0:T(8,128)(2,1)S(1)} %bitcast.82), custom_call_target="tpu_custom_call" | custom-call | flops 268435456 | bytes 4194304 | tf_op jit(solution)/shard_map/pallas_call | solution.py:288
  22.6 0.0 copy-done.2
  22.6 0.1 copy.29
  22.7 1.6 %collective-permute-start.2 = (bf16[512,128]{1,0:T(8,128)(2,1)}, bf16[512,128]{1,0:T(8,128)(2,1)S(1)}, u32[]{:S(2)}, u32[]{:S(2)}) collective-permute-start(bf16[512,128]{1,0:T(8,128)(2,1)} %get-tuple-element.20), channel_id=1, source_target_pairs={{0,0},{1,1},{2,38},{3,39},{4,76},{5,77},{6,100},{7,101},{8,142},{9... | collective-permute-start | bytes 393224 | tf_op jit(solution)/shard_map/ppermute | solution.py:301
  24.3 0.7 collective-permute-start.1
  25.0 0.0 copy-done.8
  25.0 0.0 copy-done.9
  25.0 0.7 pad_maximum_fusion.1
  25.7 20.3 %all-to-all-start.1 = ((bf16[32,8,256]{2,1,0:T(8,128)(2,1)}), bf16[32,8,256]{2,1,0:T(8,128)(2,1)S(1)}, u32[]{:S(2)}, u32[]{:S(2)}) async-start(bf16[32,8,256]{2,1,0:T(8,128)(2,1)} %pad_maximum_fusion.1), calls=%async_computation.1 | async-start | bytes 262144 | tf_op jit(solution)/shard_map/all_to_all | solution.py:313
  46.0 0.0 copy-done.4
  46.1 1.3 %shard_map.94.outer_ref = bf16[1024,1024]{1,0:T(8,128)(2,1)S(1)} custom-call(s32[1]{0:T(128)} %bitcast.core_ref, bf16[256,512]{1,0:T(8,128)(2,1)S(1)} %bitcast.84, bf16[32,16,128]{2,1,0:T(8,128)(2,1)S(1)} %copy-done.4, bf16[32,16,128]{2,1,0:T(8,128)(2,1)S(1)} %collective-permute-done.other_ref), custom_call_target="tpu_custom_call" | custom-call | flops 8589934592 | bytes 4194304 | tf_op jit(solution)/shard_map/pallas_call | solution.py:310
  47.4 0.0 collective-permute-done.2.right_ref
  47.4 0.0 collective-permute-done.1.factors_ref
  47.4 1.4 %shard_map.95 = bf16[32,32,128]{2,1,0:T(8,128)(2,1)} custom-call(bf16[1024,1024]{1,0:T(8,128)(2,1)S(1)} %shard_map.94.outer_ref, bf16[512,128]{1,0:T(8,128)(2,1)S(1)} %collective-permute-done.1.factors_ref, bf16[512,128]{1,0:T(8,128)(2,1)S(1)} %collective-permute-done.2.right_ref), custom_call_target="tpu_custom_call" | custom-call | flops 268435456 | bytes 4194304 | tf_op jit(solution)/shard_map/pallas_call | solution.py:318
  48.8 5.8 %all-to-all-done.1 = bf16[32,8,256]{2,1,0:T(8,128)(2,1)S(1)} async-done(((bf16[32,8,256]{2,1,0:T(8,128)(2,1)}), bf16[32,8,256]{2,1,0:T(8,128)(2,1)S(1)}, u32[]{:S(2)}, u32[]{:S(2)}) %all-to-all-start.1) | async-done | bytes 131104 | tf_op jit(solution)/shard_map/all_to_all | solution.py:313
  54.6 9.5 %all-to-all-start.2 = ((bf16[32,32,128]{2,1,0:T(8,128)(2,1)}), bf16[32,32,128]{2,1,0:T(8,128)(2,1)S(1)}, u32[]{:S(2)}, u32[]{:S(2)}) async-start(bf16[32,32,128]{2,1,0:T(8,128)(2,1)} %shard_map.95), calls=%async_computation.2 | async-start | bytes 524288 | tf_op jit(solution)/shard_map/all_to_all | solution.py:321
  64.2 0.0 copy-done
  64.2 0.2 convolution_convert_fusion
  64.4 0.2 copy.32
  64.6 0.0 copy-start.10
  64.6 0.0 copy-start.7
  64.6 0.3 fusion.21
  65.0 10.2 %all-to-all-done.2 = bf16[32,32,128]{2,1,0:T(8,128)(2,1)S(1)} async-done(((bf16[32,32,128]{2,1,0:T(8,128)(2,1)}), bf16[32,32,128]{2,1,0:T(8,128)(2,1)S(1)}, u32[]{:S(2)}, u32[]{:S(2)}) %all-to-all-start.2) | async-done | bytes 262176 | tf_op jit(solution)/shard_map/all_to_all | solution.py:321
  75.2 0.2 reshape.54
  75.4 0.6 reduce_sum.30
  76.0 0.1 copy.30
  76.1 0.1 copy.31
  76.2 0.1 reshape.56
  76.3 0.0 copy-done.10
  76.3 0.1 fusion.11
  76.5 0.0 copy-done.7
  76.5 0.2 fusion.37
  76.7 0.3 fusion.27
  76.9 0.2 fusion.12
  77.2 0.3 fusion.13
  77.5 0.3 fusion.14
  77.7 0.2 fusion.15
  78.0 0.3 fusion.10
  78.3 11.4 %all_to_all.20 = bf16[32,4,256]{2,1,0:T(4,128)(2,1)S(1)} all-to-all(bf16[32,4,256]{2,1,0:T(4,128)(2,1)S(1)} %reshape.60), channel_id=1, replica_groups=mesh['ri'=16,'rj'=32] {'rj'}, dimensions={0} | all-to-all | bytes 131072 | tf_op jit(solution)/shard_map/all_to_all | solution.py:335
  89.7 0.6 copy.47
  (6 shorter events, 0.2 us)
Async XLA Ops:
  0.0 64.2 %copy-start = (bf16[256,1024]{1,0:T(8,128)(2,1)S(1)}, bf16[256,1024]{1,0:T(8,128)(2,1)}, u32[]{:S(2)}) copy-start(bf16[256,1024]{1,0:T(8,128)(2,1)} %param.16) | copy-start | bytes 1572868
  0.0 0.8 copy-start.5
  0.8 0.7 copy-start.6
  2.7 18.4 %all-to-all-start = ((bf16[16,8,1024]{2,1,0:T(8,128)(2,1)}), bf16[16,8,1024]{2,1,0:T(8,128)(2,1)S(1)}, u32[]{:S(2)}, u32[]{:S(2)}) async-start(bf16[16,8,1024]{2,1,0:T(8,128)(2,1)} %bitcast.1), calls=%async_computation | async-start | bytes 524288 | tf_op jit(solution)/shard_map/all_to_all | solution.py:275
  11.9 4.3 %collective-permute-start = (bf16[32,16,128]{2,1,0:T(8,128)(2,1)}, bf16[32,16,128]{2,1,0:T(8,128)(2,1)S(1)}, u32[]{:S(2)}, u32[]{:S(2)}) collective-permute-start(bf16[32,16,128]{2,1,0:T(8,128)(2,1)} %own_ref.2), channel_id=1, source_target_pairs={{0,1},{1,0},{2,3},{3,2},{4,5},{5,4},{6,7},{7,6},{8,9},{9,8},{10,11... | collective-permute-start | bytes 393224 | tf_op jit(solution)/shard_map/ppermute | solution.py:284
  16.2 0.9 %copy-start.1 = (bf16[1024,128]{1,0:T(8,128)(2,1)S(1)}, bf16[1024,128]{1,0:T(8,128)(2,1)}, u32[]{:S(2)}) copy-start(bf16[1024,128]{1,0:T(8,128)(2,1)} %map_ref.1) | copy-start | bytes 786436
  17.1 0.9 %copy-start.3 = (bf16[32,16,128]{2,1,0:T(8,128)(2,1)S(1)}, bf16[32,16,128]{2,1,0:T(8,128)(2,1)}, u32[]{:S(2)}) copy-start(bf16[32,16,128]{2,1,0:T(8,128)(2,1)} %own_ref.2) | copy-start | bytes 393220
  19.9 2.7 %copy-start.2 = (bf16[1024,128]{1,0:T(8,128)(2,1)S(1)}, bf16[1024,128]{1,0:T(8,128)(2,1)}, u32[]{:S(2)}) copy-start(bf16[1024,128]{1,0:T(8,128)(2,1)} %map_ref.1) | copy-start | bytes 786436
  19.9 26.1 %copy-start.4 = (bf16[32,16,128]{2,1,0:T(8,128)(2,1)S(1)}, bf16[32,16,128]{2,1,0:T(8,128)(2,1)}, u32[]{:S(2)}) copy-start(bf16[32,16,128]{2,1,0:T(8,128)(2,1)} %own_ref.2) | copy-start | bytes 393220
  21.1 3.9 %copy-start.8 = (bf16[32,4,256]{2,1,0:T(4,128)(2,1)S(1)}, bf16[32,4,256]{2,1,0:T(4,128)(2,1)}, u32[]{:S(2)}) copy-start(bf16[32,4,256]{2,1,0:T(4,128)(2,1)} %param.12) | copy-start | bytes 196612
  21.1 3.9 %copy-start.9 = (bf16[32,4,256]{2,1,0:T(4,128)(2,1)S(1)}, bf16[32,4,256]{2,1,0:T(4,128)(2,1)}, u32[]{:S(2)}) copy-start(bf16[32,4,256]{2,1,0:T(4,128)(2,1)} %param.13) | copy-start | bytes 196612
  22.7 24.7 %collective-permute-start.2 = (bf16[512,128]{1,0:T(8,128)(2,1)}, bf16[512,128]{1,0:T(8,128)(2,1)S(1)}, u32[]{:S(2)}, u32[]{:S(2)}) collective-permute-start(bf16[512,128]{1,0:T(8,128)(2,1)} %get-tuple-element.20), channel_id=1, source_target_pairs={{0,0},{1,1},{2,38},{3,39},{4,76},{5,77},{6,100},{7,101},{8,142},{9... | collective-permute-start | bytes 393224 | tf_op jit(solution)/shard_map/ppermute | solution.py:301
  24.3 23.1 %collective-permute-start.1 = (bf16[512,128]{1,0:T(8,128)(2,1)S(1)}, bf16[512,128]{1,0:T(8,128)(2,1)S(1)}, u32[]{:S(2)}, u32[]{:S(2)}) collective-permute-start(bf16[512,128]{1,0:T(8,128)(2,1)S(1)} %get-tuple-element.19), channel_id=1, source_target_pairs={{0,0},{1,1},{38,2},{39,3},{76,4},{77,5},{100,6},{101,7},{142,8},{1... | collective-permute-start | bytes 393224 | tf_op jit(solution)/shard_map/ppermute | solution.py:296
  25.7 28.9 %all-to-all-start.1 = ((bf16[32,8,256]{2,1,0:T(8,128)(2,1)}), bf16[32,8,256]{2,1,0:T(8,128)(2,1)S(1)}, u32[]{:S(2)}, u32[]{:S(2)}) async-start(bf16[32,8,256]{2,1,0:T(8,128)(2,1)} %pad_maximum_fusion.1), calls=%async_computation.1 | async-start | bytes 262144 | tf_op jit(solution)/shard_map/all_to_all | solution.py:313
  54.6 20.6 %all-to-all-start.2 = ((bf16[32,32,128]{2,1,0:T(8,128)(2,1)}), bf16[32,32,128]{2,1,0:T(8,128)(2,1)S(1)}, u32[]{:S(2)}, u32[]{:S(2)}) async-start(bf16[32,32,128]{2,1,0:T(8,128)(2,1)} %shard_map.95), calls=%async_computation.2 | async-start | bytes 524288 | tf_op jit(solution)/shard_map/all_to_all | solution.py:321
  64.6 11.7 %copy-start.10 = (bf16[256,64]{0,1:T(8,128)(2,1)S(1)}, bf16[256,64]{0,1:T(8,128)(2,1)}, u32[]{:S(2)}) copy-start(bf16[256,64]{0,1:T(8,128)(2,1)} %param.15) | copy-start | bytes 98308
  64.6 11.8 %copy-start.7 = (bf16[256,256]{1,0:T(8,128)(2,1)S(1)}, bf16[256,256]{1,0:T(8,128)(2,1)}, u32[]{:S(2)}) copy-start(bf16[256,256]{1,0:T(8,128)(2,1)} %param.17) | copy-start | bytes 393220
